TPU v7x, 256 devices: a whole 4x4x8 slice. The times are simulated.
256 devices in a mesh: row: 32 (over x, z_lo, core), col: 8 (over y, z_hi).
Axes of the slice: x: 4, y: 4, z: 8 (z_hi: 2, z_lo: 4; z = z_hi * 4 + z_lo), core: 2. Of those that a mesh axis runs over, the one named last changes fastest.
Arguments:
- root_inverse: float32 [4096, 4096], P('row', 'col'), as said below
- factor_blocks: float32 [2, 4096, 2048], P(None, 'row', 'col'), may hold values from -0.1875 to 0.1875
- pattern: int32 [2, 32], replicated, may hold values 0 or 1
- diag_inverse: float32 [2, 2048, 2048], P(None, 'row', 'col'), may hold values from -0.6 to 0.6
Outputs:
- cross_inverse: float32 [2, 4096, 2048], P(None, 'row', 'col')
- diag_block_inverse: float32 [2, 2048, 2048], P(None, 'row', 'col')
Inputs may be any that keep to these rules, and one draw needn't show every extreme that they name: root_inverse is symmetric.
All inputs are finite; a program needn't handle non-finite values.
Results may differ from a plain program's by a relative error of at most 0.000098.
Values sent between devices are 32-bit elements; how exact they have to be, the bound alone decides.
No kernel may reach another device: no remote copies, remote signals or barrier semaphores. Data moves between devices by JAX's collectives and lax.ppermute only.
A program may use at most 64 MiB of HBM per device.

v0:
```python
import jax
import jax.numpy as jnp
from jax import lax
from jax.experimental import pallas as pl
from jax.experimental.pallas import tpu as pltpu
from jax.sharding import PartitionSpec as P

AX = ("row", "col")
BLK = 128
NX, NZL, NC, NY, NZH = 4, 4, 2, 4, 2


def linear(x, zl, c, y, zh):
    return (((x * NZL + zl) * NC + c) * NY + y) * NZH + zh


def moves(target):
    pairs = []
    for x in range(NX):
        for zl in range(NZL):
            for c in range(NC):
                for y in range(NY):
                    for zh in range(NZH):
                        pairs.append((linear(x, zl, c, y, zh), linear(*target(x, zl, c, y, zh))))
    return pairs


def z_step(d):
    def target(x, zl, c, y, zh):
        z = (zh * NZL + zl + d) % (NZL * NZH)
        return x, z % NZL, c, y, z // NZL

    return moves(target)


Z_UP, Z_DOWN = z_step(1), z_step(-1)
Z_MOVES = [moves(lambda x, zl, c, y, zh, d=d: (x, (zl + d) % NZL, c, y, zh)) for d in range(NZL)]
X_MOVES = [moves(lambda x, zl, c, y, zh, d=d: ((x + d) % NX, zl, c, y, zh)) for d in range(NX)]
Y_MOVES = [moves(lambda x, zl, c, y, zh, d=d: (x, zl, c, (y + d) % NY, zh)) for d in range(NY)]
CORE = moves(lambda x, zl, c, y, zh: (x, zl, 1 - c, y, zh))
CROSS = [moves(lambda x, zl, c, y, zh, t=t: ((y + t) % NX, zl, c, x, zh)) for t in range(NX)]
HOME = moves(lambda x, zl, c, y, zh: (x, (zh * NZL + zl) >> 1, zl & 1, y, c))


def send(value, pairs):
    return lax.ppermute(value, AX, pairs)


def step(pair):
    return send(pair[0], Z_UP), send(pair[1], Z_DOWN)


def last_step(pair):
    half = pair[0].shape[0] // 2
    return send(pair[0][:half], Z_UP), send(pair[1][half:], Z_DOWN)


def in_order(block, one, two, three, four):
    return [block, one[1], two[1], three[1], four[0], four[1], three[0], two[0], one[0]]


def split(v):
    hi = v.astype(jnp.bfloat16)
    return hi, (v - hi.astype(jnp.float32)).astype(jnp.bfloat16)


def dot3(a, b, dims):
    def one(p, q):
        return lax.dot_general(p, q, (dims, ((), ())), preferred_element_type=jnp.float32)

    return one(a[0], b[0]) + (one(a[0], b[1]) + one(a[1], b[0]))


def factor_kernel(at, pattern, blocks, factor, p0, p1, p2, p3, pieces):
    row, zl = at[4], at[5]
    cols = blocks.shape[2]
    for child in range(2):
        weight = pattern[child, row].astype(jnp.float32)
        masked = blocks[child] * weight
        factor[:, child * cols : (child + 1) * cols] = masked
        for q in range(4):
            pieces[q, :, child * 64 : (child + 1) * 64] = masked[:, q * 64 : (q + 1) * 64]
    for d, ref in enumerate((p0, p1, p2, p3)):
        ref[...] = pieces[(zl + d) & 3]


def cross_kernel(at, r0, r1, r2, r3, r4t, r4b, r5, r6, r7, o0, o1, o2, o3, s0, s1, s2, s3, t0, t1, t2, t3, hi, lo, total):
    x, y, z, c, zl = at[0], at[1], at[2], at[3], at[5]
    for t, (own, other) in enumerate(((o0, s0), (o1, s1), (o2, s2), (o3, s3))):
        here = slice(t * BLK, (t + 1) * BLK)
        for ref, core in ((own, c), (other, 1 - c)):
            for d in range(4):
                rows = pl.ds(pl.multiple_of((((zl - d) & 3) * 2 + core) * BLK, BLK), BLK)
                hi[rows, here], lo[rows, here] = split(ref[d])
    blocks = [(r0, None), (r1, None), (r2, None), (r3, None), (r4t, r4b), (r5, None), (r6, None), (r7, None)]

    def product(d):
        place = (z + d) & 7
        start = pl.multiple_of((place >> 2) * (4 * BLK), 4 * BLK)
        f = hi[pl.ds(start, 4 * BLK), :], lo[pl.ds(start, 4 * BLK), :]
        first, second = blocks[d]
        value = first[...] if second is None else jnp.concatenate([first[...], second[...]], axis=0)
        return dot3(split(value), f, ((1,), (0,)))

    for p in range(4):
        value = product(p) + product(p + 4)
        rows = pl.ds(pl.multiple_of(((z + p) & 3) * BLK, BLK), BLK)
        for t in range(4):
            total[t, rows, :] = value[:, t * BLK : (t + 1) * BLK]
    for d, ref in enumerate((t0, t1, t2, t3)):
        ref[...] = total[(x - y - d) & 3]


def diag_kernel(at, e0, e1, e2, e3, e4t, e4b, e5, e6, e7, g0, g1, g2, g3, out_send, out_keep, fh, fl, gh, gl, total):
    x, y, z, c = at[0], at[1], at[2], at[3]
    half = BLK // 2
    for ref, d, skip in ((e0, 0, 0), (e1, 1, 0), (e2, 2, 0), (e3, 3, 0), (e4t, 4, 0), (e4b, 4, half), (e5, 5, 0), (e6, 6, 0), (e7, 7, 0)):
        rows = pl.ds(pl.multiple_of(((z + d) & 7) * BLK + skip, half), ref.shape[0])
        fh[rows, :], fl[rows, :] = split(ref[...])
    for d, ref in enumerate((g0, g1, g2, g3)):
        h, l = split(ref[...])
        for child in range(2):
            to = slice(child * 256 + d * 64, child * 256 + (d + 1) * 64)
            of = slice(child * 64, (child + 1) * 64)
            gh[:, to], gl[:, to] = h[:, of], l[:, of]
    for child in range(2):
        here = slice(child * 256, (child + 1) * 256)
        g = gh[:, here], gl[:, here]
        for h in range(2):
            rows = slice(h * 4 * BLK, (h + 1) * 4 * BLK)
            value = dot3(g, (fh[rows, here], fl[rows, here]), ((0,), (0,)))
            for d in range(4):
                total[h, d, child] = value[d * 64 : (d + 1) * 64, :]
    for t in range(4):
        d = (y - x - t) & 3
        out_keep[t] = total[c, d]
        out_send[t] = total[1 - c, d]


def output_kernel(at, pattern, a0, a1, a2, a3, out, pieces):
    row, zl = at[4], at[5]
    for d, ref in enumerate((a0, a1, a2, a3)):
        pieces[(zl - d) & 3] = ref[...]
    for child in range(2):
        weight = pattern[child, row].astype(jnp.float32)
        for q in range(4):
            out[child, :, q * 64 : (q + 1) * 64] = -(pieces[q, :, child * 64 : (child + 1) * 64] * weight)


def local_call(kernel, scalars, operands, outs, scratch, flops, moved):
    vmem, smem = pl.BlockSpec(memory_space=pltpu.VMEM), pl.BlockSpec(memory_space=pltpu.SMEM)
    return pl.pallas_call(
        kernel,
        out_shape=[jax.ShapeDtypeStruct(s, jnp.float32) for s in outs],
        in_specs=[smem] * len(scalars) + [vmem] * len(operands),
        out_specs=[vmem] * len(outs),
        scratch_shapes=scratch,
        cost_estimate=pl.CostEstimate(flops=flops, bytes_accessed=moved, transcendentals=0),
        compiler_params=pltpu.CompilerParams(vmem_limit_bytes=32 * 2**20),
    )(*scalars, *operands)


def body(root_inverse, factor_blocks, pattern, diag_inverse):
    row, col = lax.axis_index("row"), lax.axis_index("col")
    x, zl, c, y, zh = row >> 3, (row >> 1) & 3, row & 1, col >> 1, col & 1
    at = jnp.stack([x, y, zh * 4 + zl, c, row, zl]).astype(jnp.int32)
    cols = factor_blocks.shape[2]
    piece = (BLK, BLK)

    root1 = step((root_inverse, root_inverse))
    factor, *strips = local_call(
        factor_kernel, [at, pattern], [factor_blocks], [(BLK, 2 * cols)] + [piece] * 4, [pltpu.VMEM((4,) + piece, jnp.float32)], 2**16, 2**20
    )
    strips[3], root1 = lax.optimization_barrier((strips[3], root1))
    column = jnp.stack([strips[0]] + [send(strips[d], Z_MOVES[d]) for d in (1, 2, 3)])
    own = [send(column, CROSS[t]) for t in range(4)]
    other = [send(v, CORE) for v in own]
    around1 = step((factor, factor))
    root2 = step(root1)
    root3 = step(root2)
    root4 = last_step(root3)
    wide = pltpu.VMEM((8 * BLK, 2 * cols), jnp.bfloat16)
    parts = local_call(
        cross_kernel,
        [at],
        in_order(root_inverse, root1, root2, root3, root4) + own + other,
        [(4 * BLK, BLK)] * 4,
        [wide, wide, pltpu.VMEM((4, 4 * BLK, BLK), jnp.float32)],
        6 * 512 * 1024 * 512,
        6 * 2**20,
    )
    around2 = step(around1)
    g = parts[0] + send(parts[1], Y_MOVES[1]) + send(parts[2], Y_MOVES[2]) + send(parts[3], Y_MOVES[3])
    around3 = step(around2)
    gathered = [g] + [send(g, Y_MOVES[d]) for d in (1, 2, 3)]
    around4 = last_step(around3)

    out_send, out_keep = local_call(
        diag_kernel,
        [at],
        in_order(factor, around1, around2, around3, around4) + gathered,
        [(4, 2, BLK // 2, cols)] * 2,
        [wide, wide]
        + [pltpu.VMEM((4 * BLK, 2 * cols), jnp.bfloat16)] * 2
        + [pltpu.VMEM((2, 4, 2, BLK // 2, cols), jnp.float32)],
        6 * 512 * 512 * 512,
        6 * 2**20,
    )
    g_rows = g.reshape((4,) + piece)
    rows = [lax.dynamic_index_in_dim(g_rows, (zl + d) & 3, 0, keepdims=False) for d in range(4)]
    rows = [rows[0]] + [send(rows[d], Z_MOVES[d]) for d in (1, 2, 3)]
    swapped = send(out_send, CORE)
    (cross,) = local_call(output_kernel, [at, pattern], rows, [(2, BLK, cols)], [pltpu.VMEM((4,) + piece, jnp.float32)], 2**16, 2**20)
    part = out_keep + swapped
    last = part[0] + send(part[1], X_MOVES[1]) + send(part[2], X_MOVES[2]) + send(part[3], X_MOVES[3])
    last, cross = lax.optimization_barrier((last, cross))
    diag = diag_inverse + send(last, HOME)
    return cross, diag


def solution(mesh):
    placed = (P("row", "col"), P(None, "row", "col"), P(), P(None, "row", "col"))
    return jax.shard_map(
        body,
        mesh=mesh,
        in_specs=placed,
        out_specs=(P(None, "row", "col"), P(None, "row", "col")),
        check_vma=False,
    )
```

profile of v0, /device:TPU:98, one launch (start us, length us, event | category | flops | bytes accessed | tf_op | source)
XLA Modules:
  0.0 116.2 jit_solution(15773456723732379302)
XLA Ops:
  0.6 3.2 %collective-permute-start.8 = (f32[128,512]{1,0:T(8,128)}, f32[128,512]{1,0:T(8,128)S(1)}, u32[]{:S(2)}, u32[]{:S(2)}) collective-permute-start(f32[128,512]{1,0:T(8,128)} %r0.1), channel_id=1, source_target_pairs={{0,16},{1,17},{2,18},{3,19},{4,20},{5,21},{6,22},{7,23},{8,24},{9,... | collective-permute-start | bytes 786440 | tf_op jit(solution)/shard_map/ppermute | solution.py:46
  3.8 0.1 stack.42.at
  3.9 0.6 copy-done.1
  4.5 0.9 copy-done
  5.5 0.7 shard_map.59
  6.2 2.1 %collective-permute-start.16 = (f32[128,128]{1,0:T(8,128)S(1)}, f32[128,128]{1,0:T(8,128)S(1)}, u32[]{:S(2)}, u32[]{:S(2)}) collective-permute-start(f32[128,128]{1,0:T(8,128)S(1)} %get-tuple-element.23), channel_id=1, source_target_pairs={{0,16},{1,17},{2,18},{3,19},{4,20},{5,21},{6,22},{7,23},{8,24},{9,... | collective-permute-start | bytes 196616 | tf_op jit(solution)/shard_map/ppermute | solution.py:46
  8.3 1.4 %collective-permute-done.8.r7 = f32[128,512]{1,0:T(8,128)S(1)} collective-permute-done((f32[128,512]{1,0:T(8,128)}, f32[128,512]{1,0:T(8,128)S(1)}, u32[]{:S(2)}, u32[]{:S(2)}) %collective-permute-start.8) | collective-permute-done | bytes 262176 | tf_op jit(solution)/shard_map/ppermute | solution.py:46
  9.7 3.3 %collective-permute-done.9.r1 = f32[128,512]{1,0:T(8,128)S(1)} collective-permute-done((f32[128,512]{1,0:T(8,128)}, f32[128,512]{1,0:T(8,128)S(1)}, u32[]{:S(2)}, u32[]{:S(2)}) %collective-permute-start.9) | collective-permute-done | bytes 262176 | tf_op jit(solution)/shard_map/ppermute | solution.py:46
  13.0 0.3 collective-permute-start.18
  13.3 2.0 %collective-permute-start.3 = (f32[128,512]{1,0:T(8,128)S(1)}, f32[128,512]{1,0:T(8,128)S(1)}, u32[]{:S(2)}, u32[]{:S(2)}) collective-permute-start(f32[128,512]{1,0:T(8,128)S(1)} %get-tuple-element.18.e0), channel_id=1, source_target_pairs={{0,16},{1,17},{2,18},{3,19},{4,20},{5,21},{6,22},{7,23},{8,24},{9,... | collective-permute-start | bytes 786440 | tf_op jit(solution)/shard_map/ppermute | solution.py:46
  15.3 1.2 %collective-permute-start.12 = (f32[128,512]{1,0:T(8,128)S(1)}, f32[128,512]{1,0:T(8,128)S(1)}, u32[]{:S(2)}, u32[]{:S(2)}) collective-permute-start(f32[128,512]{1,0:T(8,128)S(1)} %collective-permute-done.8.r7), channel_id=1, source_target_pairs={{0,16},{1,17},{2,18},{3,19},{4,20},{5,21},{6,22},{7,23},{8,24},{9,... | collective-permute-start | bytes 786440 | tf_op jit(solution)/shard_map/ppermute | solution.py:46
  16.5 0.0 collective-permute-done.16
  16.5 0.8 collective-permute-start.10
  17.4 0.0 collective-permute-done.17
  17.4 2.5 %collective-permute-done.18 = f32[128,128]{1,0:T(8,128)S(1)} collective-permute-done((f32[128,128]{1,0:T(8,128)S(1)}, f32[128,128]{1,0:T(8,128)S(1)}, u32[]{:S(2)}, u32[]{:S(2)}) %collective-permute-start.18) | collective-permute-done | bytes 65568 | tf_op jit(solution)/shard_map/ppermute | solution.py:46
  19.9 0.0 copy-start.2
  19.9 3.6 %collective-permute-start.19 = (f32[4,128,128]{2,1,0:T(8,128)S(1)}, f32[4,128,128]{2,1,0:T(8,128)S(1)}, u32[]{:S(2)}, u32[]{:S(2)}) collective-permute-start(f32[4,128,128]{2,1,0:T(8,128)S(1)} %pad_maximum_fusion), channel_id=1, source_target_pairs={{0,0},{1,1},{2,64},{3,65},{4,128},{5,129},{6,192},{7,193},{8,8},{9... | collective-permute-start | bytes 786440 | tf_op jit(solution)/shard_map/ppermute | solution.py:46
  23.5 0.1 collective-permute-start.20
  23.6 2.6 %collective-permute-start.21 = (f32[4,128,128]{2,1,0:T(8,128)S(1)}, f32[4,128,128]{2,1,0:T(8,128)S(1)}, u32[]{:S(2)}, u32[]{:S(2)}) collective-permute-start(f32[4,128,128]{2,1,0:T(8,128)S(1)} %pad_maximum_fusion), channel_id=1, source_target_pairs={{0,128},{1,129},{2,192},{3,193},{4,0},{5,1},{6,64},{7,65},{8,136},... | collective-permute-start | bytes 786440 | tf_op jit(solution)/shard_map/ppermute | solution.py:46
  26.2 0.7 collective-permute-done.12.r6
  26.9 3.4 %collective-permute-start.22 = (f32[4,128,128]{2,1,0:T(8,128)S(1)}, f32[4,128,128]{2,1,0:T(8,128)S(1)}, u32[]{:S(2)}, u32[]{:S(2)}) collective-permute-start(f32[4,128,128]{2,1,0:T(8,128)S(1)} %pad_maximum_fusion), channel_id=1, source_target_pairs={{0,192},{1,193},{2,0},{3,1},{4,64},{5,65},{6,128},{7,129},{8,200},... | collective-permute-start | bytes 786440 | tf_op jit(solution)/shard_map/ppermute | solution.py:46
  30.4 1.8 %collective-permute-start.13 = (f32[128,512]{1,0:T(8,128)S(1)}, f32[128,512]{1,0:T(8,128)S(1)}, u32[]{:S(2)}, u32[]{:S(2)}) collective-permute-start(f32[128,512]{1,0:T(8,128)S(1)} %collective-permute-done.12.r6), channel_id=1, source_target_pairs={{0,16},{1,17},{2,18},{3,19},{4,20},{5,21},{6,22},{7,23},{8,24},{9,... | collective-permute-start | bytes 786440 | tf_op jit(solution)/shard_map/ppermute | solution.py:46
  32.2 0.1 collective-permute-done.19.o0
  32.3 0.1 collective-permute-start.11
  32.4 0.2 collective-permute-done.20.o1
  32.6 0.4 collective-permute-start
  33.1 2.0 %collective-permute-done.21.o2 = f32[4,128,128]{2,1,0:T(8,128)S(1)} collective-permute-done((f32[4,128,128]{2,1,0:T(8,128)S(1)}, f32[4,128,128]{2,1,0:T(8,128)S(1)}, u32[]{:S(2)}, u32[]{:S(2)}) %collective-permute-start.21) | collective-permute-done | bytes 262176 | tf_op jit(solution)/shard_map/ppermute | solution.py:46
  35.0 6.0 %collective-permute-done.22.o3 = f32[4,128,128]{2,1,0:T(8,128)S(1)} collective-permute-done((f32[4,128,128]{2,1,0:T(8,128)S(1)}, f32[4,128,128]{2,1,0:T(8,128)S(1)}, u32[]{:S(2)}, u32[]{:S(2)}) %collective-permute-start.22) | collective-permute-done | bytes 262176 | tf_op jit(solution)/shard_map/ppermute | solution.py:46
  41.0 0.5 collective-permute-start.25
  41.5 0.1 collective-permute-done.11.r3
  41.7 2.8 %collective-permute-done.e1 = f32[128,512]{1,0:T(8,128)S(1)} collective-permute-done((f32[128,512]{1,0:T(8,128)S(1)}, f32[128,512]{1,0:T(8,128)S(1)}, u32[]{:S(2)}, u32[]{:S(2)}) %collective-permute-start) | collective-permute-done | bytes 262176 | tf_op jit(solution)/shard_map/ppermute | solution.py:46
  44.4 2.0 %collective-permute-start.15 = (f32[64,512]{1,0:T(8,128)S(1)}, f32[64,512]{1,0:T(8,128)S(1)}, u32[]{:S(2)}, u32[]{:S(2)}) collective-permute-start(f32[64,512]{1,0:T(8,128)S(1)} %slice.35), channel_id=1, source_target_pairs={{0,49},{1,48},{2,51},{3,50},{4,53},{5,52},{6,55},{7,54},{8,57},{9,... | collective-permute-start | bytes 393224 | tf_op jit(solution)/shard_map/ppermute | solution.py:46
  46.5 1.2 %collective-permute-start.4 = (f32[128,512]{1,0:T(8,128)S(1)}, f32[128,512]{1,0:T(8,128)S(1)}, u32[]{:S(2)}, u32[]{:S(2)}) collective-permute-start(f32[128,512]{1,0:T(8,128)S(1)} %collective-permute-done.3.e7), channel_id=1, source_target_pairs={{0,16},{1,17},{2,18},{3,19},{4,20},{5,21},{6,22},{7,23},{8,24},{9,... | collective-permute-start | bytes 786440 | tf_op jit(solution)/shard_map/ppermute | solution.py:46
  47.7 0.8 collective-permute-start.1
  48.5 2.3 %collective-permute-done.14.r4t = f32[64,512]{1,0:T(8,128)S(1)} collective-permute-done((f32[64,512]{1,0:T(8,128)S(1)}, f32[64,512]{1,0:T(8,128)S(1)}, u32[]{:S(2)}, u32[]{:S(2)}) %collective-permute-start.14) | collective-permute-done | bytes 131104 | tf_op jit(solution)/shard_map/ppermute | solution.py:46
  50.9 3.0 %shard_map.60 = (f32[512,128]{1,0:T(8,128)S(1)}, f32[512,128]{1,0:T(8,128)S(1)}, f32[512,128]{1,0:T(8,128)S(1)}, f32[512,128]{1,0:T(8,128)S(1)}) custom-call(s32[6]{0:T(128)S(1)} %stack.42.at, f32[128,512]{1,0:T(8,128)S(1)} %copy-done.2, f32[128,512]{1,0:T(8,128)S(1)} %collective-permute-done.9.r1, f32[128,512]{1,0:T(8,128)S(1)} %collective-permute-done.10.r2, ...), custom_call_target="tpu_custom_call" | custom-call | flops 1610612736 | bytes 6291456 | tf_op jit(solution)/shard_map/pallas_call | solution.py:152
  53.8 1.2 %collective-permute-start.27 = (f32[512,128]{1,0:T(8,128)S(1)}, f32[512,128]{1,0:T(8,128)S(1)}, u32[]{:S(2)}, u32[]{:S(2)}) collective-permute-start(f32[512,128]{1,0:T(8,128)S(1)} %get-tuple-element.27), channel_id=1, source_target_pairs={{0,2},{1,3},{2,4},{3,5},{4,6},{5,7},{6,0},{7,1},{8,10},{9,11},{10,... | collective-permute-start | bytes 786440 | tf_op jit(solution)/shard_map/ppermute | solution.py:46
  55.1 6.0 %collective-permute-start.28 = (f32[512,128]{1,0:T(8,128)S(1)}, f32[512,128]{1,0:T(8,128)S(1)}, u32[]{:S(2)}, u32[]{:S(2)}) collective-permute-start(f32[512,128]{1,0:T(8,128)S(1)} %get-tuple-element.28), channel_id=1, source_target_pairs={{0,4},{1,5},{2,6},{3,7},{4,0},{5,1},{6,2},{7,3},{8,12},{9,13},{10,... | collective-permute-start | bytes 786440 | tf_op jit(solution)/shard_map/ppermute | solution.py:46
  61.1 0.1 collective-permute-start.5
  61.2 1.9 %collective-permute-start.2 = (f32[128,512]{1,0:T(8,128)S(1)}, f32[128,512]{1,0:T(8,128)S(1)}, u32[]{:S(2)}, u32[]{:S(2)}) collective-permute-start(f32[128,512]{1,0:T(8,128)S(1)} %collective-permute-done.1.e2), channel_id=1, source_target_pairs={{0,49},{1,48},{2,51},{3,50},{4,53},{5,52},{6,55},{7,54},{8,57},{9,... | collective-permute-start | bytes 786440 | tf_op jit(solution)/shard_map/ppermute | solution.py:46
  63.1 2.4 %collective-permute-done.27 = f32[512,128]{1,0:T(8,128)S(1)} collective-permute-done((f32[512,128]{1,0:T(8,128)S(1)}, f32[512,128]{1,0:T(8,128)S(1)}, u32[]{:S(2)}, u32[]{:S(2)}) %collective-permute-start.27) | collective-permute-done | bytes 262176 | tf_op jit(solution)/shard_map/ppermute | solution.py:46
  65.5 3.9 %collective-permute-done.28 = f32[512,128]{1,0:T(8,128)S(1)} collective-permute-done((f32[512,128]{1,0:T(8,128)S(1)}, f32[512,128]{1,0:T(8,128)S(1)}, u32[]{:S(2)}, u32[]{:S(2)}) %collective-permute-start.28) | collective-permute-done | bytes 262176 | tf_op jit(solution)/shard_map/ppermute | solution.py:46
  69.5 0.1 collective-permute-start.30
  69.6 3.2 %collective-permute-start.31 = (f32[512,128]{1,0:T(8,128)S(1)}, f32[512,128]{1,0:T(8,128)S(1)}, u32[]{:S(2)}, u32[]{:S(2)}) collective-permute-start(f32[512,128]{1,0:T(8,128)S(1)} %add_add_fusion.g0), channel_id=1, source_target_pairs={{0,4},{1,5},{2,6},{3,7},{4,0},{5,1},{6,2},{7,3},{8,12},{9,13},{10,... | collective-permute-start | bytes 786440 | tf_op jit(solution)/shard_map/ppermute | solution.py:46
  72.8 0.7 collective-permute-start.32
  73.6 0.3 collective-permute-start.6
  73.9 2.1 %collective-permute-start.7 = (f32[64,512]{1,0:T(8,128)S(1)}, f32[64,512]{1,0:T(8,128)S(1)}, u32[]{:S(2)}, u32[]{:S(2)}) collective-permute-start(f32[64,512]{1,0:T(8,128)S(1)} %slice.33), channel_id=1, source_target_pairs={{0,49},{1,48},{2,51},{3,50},{4,53},{5,52},{6,55},{7,54},{8,57},{9,... | collective-permute-start | bytes 393224 | tf_op jit(solution)/shard_map/ppermute | solution.py:46
  76.0 2.8 %collective-permute-done.6.e4t = f32[64,512]{1,0:T(8,128)S(1)} collective-permute-done((f32[64,512]{1,0:T(8,128)S(1)}, f32[64,512]{1,0:T(8,128)S(1)}, u32[]{:S(2)}, u32[]{:S(2)}) %collective-permute-start.6) | collective-permute-done | bytes 131104 | tf_op jit(solution)/shard_map/ppermute | solution.py:46
  78.8 1.3 %collective-permute-done.7.e4b = f32[64,512]{1,0:T(8,128)S(1)} collective-permute-done((f32[64,512]{1,0:T(8,128)S(1)}, f32[64,512]{1,0:T(8,128)S(1)}, u32[]{:S(2)}, u32[]{:S(2)}) %collective-permute-start.7) | collective-permute-done | bytes 131104 | tf_op jit(solution)/shard_map/ppermute | solution.py:46
  80.2 0.7 collective-permute-done.32.g3
  80.9 2.9 %shard_map.61 = (f32[4,2,64,256]{3,2,1,0:T(8,128)S(1)}, f32[4,2,64,256]{3,2,1,0:T(8,128)S(1)}) custom-call(s32[6]{0:T(128)S(1)} %stack.42.at, f32[128,512]{1,0:T(8,128)S(1)} %get-tuple-element.18.e0, f32[128,512]{1,0:T(8,128)S(1)} %collective-permute-done.e1, f32[128,512]{1,0:T(8,128)S(1)} %collective-permute-done.1.e2, ...), custom_call_target="tpu_custom_call" | custom-call | flops 805306368 | bytes 6291456 | tf_op jit(solution)/shard_map/pallas_call | solution.py:152
  83.7 0.1 collective-permute-start.33
  83.9 0.6 collective-permute-start.37
  84.5 1.3 %collective-permute-done.33 = f32[4,2,64,256]{3,2,1,0:T(8,128)S(1)} collective-permute-done((f32[4,2,64,256]{3,2,1,0:T(8,128)S(1)}, f32[4,2,64,256]{3,2,1,0:T(8,128)S(1)}, u32[]{:S(2)}, u32[]{:S(2)}) %collective-permute-start.33) | collective-permute-done | bytes 524320 | tf_op jit(solution)/shard_map/ppermute | solution.py:46
  85.7 0.1 add.53
  85.9 2.4 %collective-permute-start.34 = (f32[2,64,256]{2,1,0:T(8,128)S(1)}, f32[2,64,256]{2,1,0:T(8,128)S(1)}, u32[]{:S(2)}, u32[]{:S(2)}) collective-permute-start(f32[2,64,256]{2,1,0:T(8,128)S(1)} %get-tuple-element.34), channel_id=1, source_target_pairs={{0,64},{1,65},{2,66},{3,67},{4,68},{5,69},{6,70},{7,71},{8,72},{9,... | collective-permute-start | bytes 393224 | tf_op jit(solution)/shard_map/ppermute | solution.py:46
  88.3 5.2 %collective-permute-start.35 = (f32[2,64,256]{2,1,0:T(8,128)S(1)}, f32[2,64,256]{2,1,0:T(8,128)S(1)}, u32[]{:S(2)}, u32[]{:S(2)}) collective-permute-start(f32[2,64,256]{2,1,0:T(8,128)S(1)} %get-tuple-element.36), channel_id=1, source_target_pairs={{0,128},{1,129},{2,130},{3,131},{4,132},{5,133},{6,134},{7,135},{8... | collective-permute-start | bytes 393224 | tf_op jit(solution)/shard_map/ppermute | solution.py:46
  93.5 2.5 %collective-permute-start.36 = (f32[2,64,256]{2,1,0:T(8,128)S(1)}, f32[2,64,256]{2,1,0:T(8,128)S(1)}, u32[]{:S(2)}, u32[]{:S(2)}) collective-permute-start(f32[2,64,256]{2,1,0:T(8,128)S(1)} %get-tuple-element.35), channel_id=1, source_target_pairs={{0,192},{1,193},{2,194},{3,195},{4,196},{5,197},{6,198},{7,199},{8... | collective-permute-start | bytes 393224 | tf_op jit(solution)/shard_map/ppermute | solution.py:46
  96.0 0.3 collective-permute-start.39
  96.3 6.5 %collective-permute-done.38.a2 = f32[128,128]{1,0:T(8,128)S(1)} collective-permute-done((f32[128,128]{1,0:T(8,128)S(1)}, f32[128,128]{1,0:T(8,128)S(1)}, u32[]{:S(2)}, u32[]{:S(2)}) %collective-permute-start.38) | collective-permute-done | bytes 65568 | tf_op jit(solution)/shard_map/ppermute | solution.py:46
  102.8 1.4 %shard_map.62 = f32[2,128,256]{2,1,0:T(8,128)} custom-call(s32[6]{0:T(128)S(1)} %stack.42.at, s32[2,32]{1,0:T(2,128)S(1)} %copy-done.1, f32[128,128]{1,0:T(8,128)S(1)} %get-tuple-element.40.a0, f32[128,128]{1,0:T(8,128)S(1)} %collective-permute-done.37.a1, f32[128,128]{1,0:T(8,128)S(1)} %collective-permute-done.38.a2, f32[128,128]{1,0:T(8,128)S(1)} %collective-permute-done.39.a3), custom_call_target="tpu_custom_call" | custom-call | flops 65536 | bytes 1048576 | tf_op jit(solution)/shard_map/pallas_call | solution.py:152
  104.3 1.9 %collective-permute-start.40 = (f32[2,64,256]{2,1,0:T(8,128)S(1)}, f32[2,64,256]{2,1,0:T(8,128)S(1)}, u32[]{:S(2)}, u32[]{:S(2)}) collective-permute-start(f32[2,64,256]{2,1,0:T(8,128)S(1)} %fusion.2), channel_id=1, source_target_pairs={{0,0},{1,32},{2,2},{3,34},{4,4},{5,36},{6,6},{7,38},{8,1},{9,33},{... | collective-permute-start | bytes 393224 | tf_op jit(solution)/shard_map/ppermute | solution.py:46
  106.2 9.3 %collective-permute-done.40 = f32[2,64,256]{2,1,0:T(8,128)S(1)} collective-permute-done((f32[2,64,256]{2,1,0:T(8,128)S(1)}, f32[2,64,256]{2,1,0:T(8,128)S(1)}, u32[]{:S(2)}, u32[]{:S(2)}) %collective-permute-start.40) | collective-permute-done | bytes 131104 | tf_op jit(solution)/shard_map/ppermute | solution.py:46
  115.6 0.7 add.64
  (42 shorter events, 0.3 us)
Async XLA Ops:
  0.6 9.1 %collective-permute-start.8 = (f32[128,512]{1,0:T(8,128)}, f32[128,512]{1,0:T(8,128)S(1)}, u32[]{:S(2)}, u32[]{:S(2)}) collective-permute-start(f32[128,512]{1,0:T(8,128)} %r0.1), channel_id=1, source_target_pairs={{0,16},{1,17},{2,18},{3,19},{4,20},{5,21},{6,22},{7,23},{8,24},{9,... | collective-permute-start | bytes 786440 | tf_op jit(solution)/shard_map/ppermute | solution.py:46
  3.8 9.2 %collective-permute-start.9 = (f32[128,512]{1,0:T(8,128)}, f32[128,512]{1,0:T(8,128)S(1)}, u32[]{:S(2)}, u32[]{:S(2)}) collective-permute-start(f32[128,512]{1,0:T(8,128)} %r0.1), channel_id=1, source_target_pairs={{0,49},{1,48},{2,51},{3,50},{4,53},{5,52},{6,55},{7,54},{8,57},{9,... | collective-permute-start | bytes 786440 | tf_op jit(solution)/shard_map/ppermute | solution.py:46
  3.8 0.7 copy-start.1
  4.5 0.9 copy-start
  6.2 10.3 %collective-permute-start.16 = (f32[128,128]{1,0:T(8,128)S(1)}, f32[128,128]{1,0:T(8,128)S(1)}, u32[]{:S(2)}, u32[]{:S(2)}) collective-permute-start(f32[128,128]{1,0:T(8,128)S(1)} %get-tuple-element.23), channel_id=1, source_target_pairs={{0,16},{1,17},{2,18},{3,19},{4,20},{5,21},{6,22},{7,23},{8,24},{9,... | collective-permute-start | bytes 196616 | tf_op jit(solution)/shard_map/ppermute | solution.py:46
  8.3 9.1 %collective-permute-start.17 = (f32[128,128]{1,0:T(8,128)S(1)}, f32[128,128]{1,0:T(8,128)S(1)}, u32[]{:S(2)}, u32[]{:S(2)}) collective-permute-start(f32[128,128]{1,0:T(8,128)S(1)} %get-tuple-element.24), channel_id=1, source_target_pairs={{0,32},{1,33},{2,34},{3,35},{4,36},{5,37},{6,38},{7,39},{8,40},{9,... | collective-permute-start | bytes 196616 | tf_op jit(solution)/shard_map/ppermute | solution.py:46
  13.0 6.8 %collective-permute-start.18 = (f32[128,128]{1,0:T(8,128)S(1)}, f32[128,128]{1,0:T(8,128)S(1)}, u32[]{:S(2)}, u32[]{:S(2)}) collective-permute-start(f32[128,128]{1,0:T(8,128)S(1)} %get-tuple-element.25), channel_id=1, source_target_pairs={{0,48},{1,49},{2,50},{3,51},{4,52},{5,53},{6,54},{7,55},{8,56},{9,... | collective-permute-start | bytes 196616 | tf_op jit(solution)/shard_map/ppermute | solution.py:46
  13.3 10.3 %collective-permute-start.3 = (f32[128,512]{1,0:T(8,128)S(1)}, f32[128,512]{1,0:T(8,128)S(1)}, u32[]{:S(2)}, u32[]{:S(2)}) collective-permute-start(f32[128,512]{1,0:T(8,128)S(1)} %get-tuple-element.18.e0), channel_id=1, source_target_pairs={{0,16},{1,17},{2,18},{3,19},{4,20},{5,21},{6,22},{7,23},{8,24},{9,... | collective-permute-start | bytes 786440 | tf_op jit(solution)/shard_map/ppermute | solution.py:46
  15.3 11.6 %collective-permute-start.12 = (f32[128,512]{1,0:T(8,128)S(1)}, f32[128,512]{1,0:T(8,128)S(1)}, u32[]{:S(2)}, u32[]{:S(2)}) collective-permute-start(f32[128,512]{1,0:T(8,128)S(1)} %collective-permute-done.8.r7), channel_id=1, source_target_pairs={{0,16},{1,17},{2,18},{3,19},{4,20},{5,21},{6,22},{7,23},{8,24},{9,... | collective-permute-start | bytes 786440 | tf_op jit(solution)/shard_map/ppermute | solution.py:46
  16.5 13.8 %collective-permute-start.10 = (f32[128,512]{1,0:T(8,128)S(1)}, f32[128,512]{1,0:T(8,128)S(1)}, u32[]{:S(2)}, u32[]{:S(2)}) collective-permute-start(f32[128,512]{1,0:T(8,128)S(1)} %collective-permute-done.9.r1), channel_id=1, source_target_pairs={{0,49},{1,48},{2,51},{3,50},{4,53},{5,52},{6,55},{7,54},{8,57},{9,... | collective-permute-start | bytes 786440 | tf_op jit(solution)/shard_map/ppermute | solution.py:46
  19.9 31.0 %copy-start.2 = (f32[128,512]{1,0:T(8,128)S(1)}, f32[128,512]{1,0:T(8,128)}, u32[]{:S(2)}) copy-start(f32[128,512]{1,0:T(8,128)} %r0.1) | copy-start | bytes 786436
  19.9 12.4 %collective-permute-start.19 = (f32[4,128,128]{2,1,0:T(8,128)S(1)}, f32[4,128,128]{2,1,0:T(8,128)S(1)}, u32[]{:S(2)}, u32[]{:S(2)}) collective-permute-start(f32[4,128,128]{2,1,0:T(8,128)S(1)} %pad_maximum_fusion), channel_id=1, source_target_pairs={{0,0},{1,1},{2,64},{3,65},{4,128},{5,129},{6,192},{7,193},{8,8},{9... | collective-permute-start | bytes 786440 | tf_op jit(solution)/shard_map/ppermute | solution.py:46
  23.5 9.1 %collective-permute-start.20 = (f32[4,128,128]{2,1,0:T(8,128)S(1)}, f32[4,128,128]{2,1,0:T(8,128)S(1)}, u32[]{:S(2)}, u32[]{:S(2)}) collective-permute-start(f32[4,128,128]{2,1,0:T(8,128)S(1)} %pad_maximum_fusion), channel_id=1, source_target_pairs={{0,64},{1,65},{2,128},{3,129},{4,192},{5,193},{6,0},{7,1},{8,72},{... | collective-permute-start | bytes 786440 | tf_op jit(solution)/shard_map/ppermute | solution.py:46
  23.6 11.4 %collective-permute-start.21 = (f32[4,128,128]{2,1,0:T(8,128)S(1)}, f32[4,128,128]{2,1,0:T(8,128)S(1)}, u32[]{:S(2)}, u32[]{:S(2)}) collective-permute-start(f32[4,128,128]{2,1,0:T(8,128)S(1)} %pad_maximum_fusion), channel_id=1, source_target_pairs={{0,128},{1,129},{2,192},{3,193},{4,0},{5,1},{6,64},{7,65},{8,136},... | collective-permute-start | bytes 786440 | tf_op jit(solution)/shard_map/ppermute | solution.py:46
  26.9 14.1 %collective-permute-start.22 = (f32[4,128,128]{2,1,0:T(8,128)S(1)}, f32[4,128,128]{2,1,0:T(8,128)S(1)}, u32[]{:S(2)}, u32[]{:S(2)}) collective-permute-start(f32[4,128,128]{2,1,0:T(8,128)S(1)} %pad_maximum_fusion), channel_id=1, source_target_pairs={{0,192},{1,193},{2,0},{3,1},{4,64},{5,65},{6,128},{7,129},{8,200},... | collective-permute-start | bytes 786440 | tf_op jit(solution)/shard_map/ppermute | solution.py:46
  30.4 10.6 %collective-permute-start.13 = (f32[128,512]{1,0:T(8,128)S(1)}, f32[128,512]{1,0:T(8,128)S(1)}, u32[]{:S(2)}, u32[]{:S(2)}) collective-permute-start(f32[128,512]{1,0:T(8,128)S(1)} %collective-permute-done.12.r6), channel_id=1, source_target_pairs={{0,16},{1,17},{2,18},{3,19},{4,20},{5,21},{6,22},{7,23},{8,24},{9,... | collective-permute-start | bytes 786440 | tf_op jit(solution)/shard_map/ppermute | solution.py:46
  32.3 9.3 %collective-permute-start.11 = (f32[128,512]{1,0:T(8,128)S(1)}, f32[128,512]{1,0:T(8,128)S(1)}, u32[]{:S(2)}, u32[]{:S(2)}) collective-permute-start(f32[128,512]{1,0:T(8,128)S(1)} %collective-permute-done.10.r2), channel_id=1, source_target_pairs={{0,49},{1,48},{2,51},{3,50},{4,53},{5,52},{6,55},{7,54},{8,57},{9,... | collective-permute-start | bytes 786440 | tf_op jit(solution)/shard_map/ppermute | solution.py:46
  32.6 11.8 %collective-permute-start = (f32[128,512]{1,0:T(8,128)S(1)}, f32[128,512]{1,0:T(8,128)S(1)}, u32[]{:S(2)}, u32[]{:S(2)}) collective-permute-start(f32[128,512]{1,0:T(8,128)S(1)} %get-tuple-element.18.e0), channel_id=1, source_target_pairs={{0,49},{1,48},{2,51},{3,50},{4,53},{5,52},{6,55},{7,54},{8,57},{9,... | collective-permute-start | bytes 786440 | tf_op jit(solution)/shard_map/ppermute | solution.py:46
  35.0 9.4 %collective-permute-start.23 = (f32[4,128,128]{2,1,0:T(8,128)S(1)}, f32[4,128,128]{2,1,0:T(8,128)S(1)}, u32[]{:S(2)}, u32[]{:S(2)}) collective-permute-start(f32[4,128,128]{2,1,0:T(8,128)S(1)} %collective-permute-done.19.o0), channel_id=1, source_target_pairs={{0,8},{1,9},{2,10},{3,11},{4,12},{5,13},{6,14},{7,15},{8,0},{9,1},... | collective-permute-start | bytes 786440 | tf_op jit(solution)/shard_map/ppermute | solution.py:46
  41.0 5.5 %collective-permute-start.24 = (f32[4,128,128]{2,1,0:T(8,128)S(1)}, f32[4,128,128]{2,1,0:T(8,128)S(1)}, u32[]{:S(2)}, u32[]{:S(2)}) collective-permute-start(f32[4,128,128]{2,1,0:T(8,128)S(1)} %collective-permute-done.20.o1), channel_id=1, source_target_pairs={{0,8},{1,9},{2,10},{3,11},{4,12},{5,13},{6,14},{7,15},{8,0},{9,1},... | collective-permute-start | bytes 786440 | tf_op jit(solution)/shard_map/ppermute | solution.py:46
  41.0 6.7 %collective-permute-start.25 = (f32[4,128,128]{2,1,0:T(8,128)S(1)}, f32[4,128,128]{2,1,0:T(8,128)S(1)}, u32[]{:S(2)}, u32[]{:S(2)}) collective-permute-start(f32[4,128,128]{2,1,0:T(8,128)S(1)} %collective-permute-done.21.o2), channel_id=1, source_target_pairs={{0,8},{1,9},{2,10},{3,11},{4,12},{5,13},{6,14},{7,15},{8,0},{9,1},... | collective-permute-start | bytes 786440 | tf_op jit(solution)/shard_map/ppermute | solution.py:46
  41.6 6.9 %collective-permute-start.26 = (f32[4,128,128]{2,1,0:T(8,128)S(1)}, f32[4,128,128]{2,1,0:T(8,128)S(1)}, u32[]{:S(2)}, u32[]{:S(2)}) collective-permute-start(f32[4,128,128]{2,1,0:T(8,128)S(1)} %collective-permute-done.22.o3), channel_id=1, source_target_pairs={{0,8},{1,9},{2,10},{3,11},{4,12},{5,13},{6,14},{7,15},{8,0},{9,1},... | collective-permute-start | bytes 786440 | tf_op jit(solution)/shard_map/ppermute | solution.py:46
  44.4 6.4 %collective-permute-start.14 = (f32[64,512]{1,0:T(8,128)S(1)}, f32[64,512]{1,0:T(8,128)S(1)}, u32[]{:S(2)}, u32[]{:S(2)}) collective-permute-start(f32[64,512]{1,0:T(8,128)S(1)} %slice.34), channel_id=1, source_target_pairs={{0,16},{1,17},{2,18},{3,19},{4,20},{5,21},{6,22},{7,23},{8,24},{9,... | collective-permute-start | bytes 393224 | tf_op jit(solution)/shard_map/ppermute | solution.py:46
  44.4 6.4 %collective-permute-start.15 = (f32[64,512]{1,0:T(8,128)S(1)}, f32[64,512]{1,0:T(8,128)S(1)}, u32[]{:S(2)}, u32[]{:S(2)}) collective-permute-start(f32[64,512]{1,0:T(8,128)S(1)} %slice.35), channel_id=1, source_target_pairs={{0,49},{1,48},{2,51},{3,50},{4,53},{5,52},{6,55},{7,54},{8,57},{9,... | collective-permute-start | bytes 393224 | tf_op jit(solution)/shard_map/ppermute | solution.py:46
  46.5 14.6 %collective-permute-start.4 = (f32[128,512]{1,0:T(8,128)S(1)}, f32[128,512]{1,0:T(8,128)S(1)}, u32[]{:S(2)}, u32[]{:S(2)}) collective-permute-start(f32[128,512]{1,0:T(8,128)S(1)} %collective-permute-done.3.e7), channel_id=1, source_target_pairs={{0,16},{1,17},{2,18},{3,19},{4,20},{5,21},{6,22},{7,23},{8,24},{9,... | collective-permute-start | bytes 786440 | tf_op jit(solution)/shard_map/ppermute | solution.py:46
  47.7 13.5 %collective-permute-start.1 = (f32[128,512]{1,0:T(8,128)S(1)}, f32[128,512]{1,0:T(8,128)S(1)}, u32[]{:S(2)}, u32[]{:S(2)}) collective-permute-start(f32[128,512]{1,0:T(8,128)S(1)} %collective-permute-done.e1), channel_id=1, source_target_pairs={{0,49},{1,48},{2,51},{3,50},{4,53},{5,52},{6,55},{7,54},{8,57},{9,... | collective-permute-start | bytes 786440 | tf_op jit(solution)/shard_map/ppermute | solution.py:46
  53.8 11.7 %collective-permute-start.27 = (f32[512,128]{1,0:T(8,128)S(1)}, f32[512,128]{1,0:T(8,128)S(1)}, u32[]{:S(2)}, u32[]{:S(2)}) collective-permute-start(f32[512,128]{1,0:T(8,128)S(1)} %get-tuple-element.27), channel_id=1, source_target_pairs={{0,2},{1,3},{2,4},{3,5},{4,6},{5,7},{6,0},{7,1},{8,10},{9,11},{10,... | collective-permute-start | bytes 786440 | tf_op jit(solution)/shard_map/ppermute | solution.py:46
  55.1 14.4 %collective-permute-start.28 = (f32[512,128]{1,0:T(8,128)S(1)}, f32[512,128]{1,0:T(8,128)S(1)}, u32[]{:S(2)}, u32[]{:S(2)}) collective-permute-start(f32[512,128]{1,0:T(8,128)S(1)} %get-tuple-element.28), channel_id=1, source_target_pairs={{0,4},{1,5},{2,6},{3,7},{4,0},{5,1},{6,2},{7,3},{8,12},{9,13},{10,... | collective-permute-start | bytes 786440 | tf_op jit(solution)/shard_map/ppermute | solution.py:46
  61.1 8.3 %collective-permute-start.29 = (f32[512,128]{1,0:T(8,128)S(1)}, f32[512,128]{1,0:T(8,128)S(1)}, u32[]{:S(2)}, u32[]{:S(2)}) collective-permute-start(f32[512,128]{1,0:T(8,128)S(1)} %get-tuple-element.29), channel_id=1, source_target_pairs={{0,6},{1,7},{2,0},{3,1},{4,2},{5,3},{6,4},{7,5},{8,14},{9,15},{10,... | collective-permute-start | bytes 786440 | tf_op jit(solution)/shard_map/ppermute | solution.py:46
  61.1 12.4 %collective-permute-start.5 = (f32[128,512]{1,0:T(8,128)S(1)}, f32[128,512]{1,0:T(8,128)S(1)}, u32[]{:S(2)}, u32[]{:S(2)}) collective-permute-start(f32[128,512]{1,0:T(8,128)S(1)} %collective-permute-done.4.e6), channel_id=1, source_target_pairs={{0,16},{1,17},{2,18},{3,19},{4,20},{5,21},{6,22},{7,23},{8,24},{9,... | collective-permute-start | bytes 786440 | tf_op jit(solution)/shard_map/ppermute | solution.py:46
  61.2 12.7 %collective-permute-start.2 = (f32[128,512]{1,0:T(8,128)S(1)}, f32[128,512]{1,0:T(8,128)S(1)}, u32[]{:S(2)}, u32[]{:S(2)}) collective-permute-start(f32[128,512]{1,0:T(8,128)S(1)} %collective-permute-done.1.e2), channel_id=1, source_target_pairs={{0,49},{1,48},{2,51},{3,50},{4,53},{5,52},{6,55},{7,54},{8,57},{9,... | collective-permute-start | bytes 786440 | tf_op jit(solution)/shard_map/ppermute | solution.py:46
  69.5 10.7 %collective-permute-start.30 = (f32[512,128]{1,0:T(8,128)S(1)}, f32[512,128]{1,0:T(8,128)S(1)}, u32[]{:S(2)}, u32[]{:S(2)}) collective-permute-start(f32[512,128]{1,0:T(8,128)S(1)} %add_add_fusion.g0), channel_id=1, source_target_pairs={{0,2},{1,3},{2,4},{3,5},{4,6},{5,7},{6,0},{7,1},{8,10},{9,11},{10,... | collective-permute-start | bytes 786440 | tf_op jit(solution)/shard_map/ppermute | solution.py:46
  69.6 10.6 %collective-permute-start.31 = (f32[512,128]{1,0:T(8,128)S(1)}, f32[512,128]{1,0:T(8,128)S(1)}, u32[]{:S(2)}, u32[]{:S(2)}) collective-permute-start(f32[512,128]{1,0:T(8,128)S(1)} %add_add_fusion.g0), channel_id=1, source_target_pairs={{0,4},{1,5},{2,6},{3,7},{4,0},{5,1},{6,2},{7,3},{8,12},{9,13},{10,... | collective-permute-start | bytes 786440 | tf_op jit(solution)/shard_map/ppermute | solution.py:46
  72.8 8.1 %collective-permute-start.32 = (f32[512,128]{1,0:T(8,128)S(1)}, f32[512,128]{1,0:T(8,128)S(1)}, u32[]{:S(2)}, u32[]{:S(2)}) collective-permute-start(f32[512,128]{1,0:T(8,128)S(1)} %add_add_fusion.g0), channel_id=1, source_target_pairs={{0,6},{1,7},{2,0},{3,1},{4,2},{5,3},{6,4},{7,5},{8,14},{9,15},{10,... | collective-permute-start | bytes 786440 | tf_op jit(solution)/shard_map/ppermute | solution.py:46
  73.6 5.3 %collective-permute-start.6 = (f32[64,512]{1,0:T(8,128)S(1)}, f32[64,512]{1,0:T(8,128)S(1)}, u32[]{:S(2)}, u32[]{:S(2)}) collective-permute-start(f32[64,512]{1,0:T(8,128)S(1)} %slice.32), channel_id=1, source_target_pairs={{0,16},{1,17},{2,18},{3,19},{4,20},{5,21},{6,22},{7,23},{8,24},{9,... | collective-permute-start | bytes 393224 | tf_op jit(solution)/shard_map/ppermute | solution.py:46
  73.9 6.3 %collective-permute-start.7 = (f32[64,512]{1,0:T(8,128)S(1)}, f32[64,512]{1,0:T(8,128)S(1)}, u32[]{:S(2)}, u32[]{:S(2)}) collective-permute-start(f32[64,512]{1,0:T(8,128)S(1)} %slice.33), channel_id=1, source_target_pairs={{0,49},{1,48},{2,51},{3,50},{4,53},{5,52},{6,55},{7,54},{8,57},{9,... | collective-permute-start | bytes 393224 | tf_op jit(solution)/shard_map/ppermute | solution.py:46
  83.7 2.0 %collective-permute-start.33 = (f32[4,2,64,256]{3,2,1,0:T(8,128)S(1)}, f32[4,2,64,256]{3,2,1,0:T(8,128)S(1)}, u32[]{:S(2)}, u32[]{:S(2)}) collective-permute-start(f32[4,2,64,256]{3,2,1,0:T(8,128)S(1)} %get-tuple-element.31), channel_id=1, source_target_pairs={{0,8},{1,9},{2,10},{3,11},{4,12},{5,13},{6,14},{7,15},{8,0},{9,1},... | collective-permute-start | bytes 1572872 | tf_op jit(solution)/shard_map/ppermute | solution.py:46
  83.9 12.2 %collective-permute-start.37 = (f32[128,128]{1,0:T(8,128)S(1)}, f32[128,128]{1,0:T(8,128)S(1)}, u32[]{:S(2)}, u32[]{:S(2)}) collective-permute-start(f32[128,128]{1,0:T(8,128)S(1)} %get-tuple-element.39), channel_id=1, source_target_pairs={{0,16},{1,17},{2,18},{3,19},{4,20},{5,21},{6,22},{7,23},{8,24},{9,... | collective-permute-start | bytes 196616 | tf_op jit(solution)/shard_map/ppermute | solution.py:46
  85.9 18.4 %collective-permute-start.34 = (f32[2,64,256]{2,1,0:T(8,128)S(1)}, f32[2,64,256]{2,1,0:T(8,128)S(1)}, u32[]{:S(2)}, u32[]{:S(2)}) collective-permute-start(f32[2,64,256]{2,1,0:T(8,128)S(1)} %get-tuple-element.34), channel_id=1, source_target_pairs={{0,64},{1,65},{2,66},{3,67},{4,68},{5,69},{6,70},{7,71},{8,72},{9,... | collective-permute-start | bytes 393224 | tf_op jit(solution)/shard_map/ppermute | solution.py:46
  88.3 15.9 %collective-permute-start.35 = (f32[2,64,256]{2,1,0:T(8,128)S(1)}, f32[2,64,256]{2,1,0:T(8,128)S(1)}, u32[]{:S(2)}, u32[]{:S(2)}) collective-permute-start(f32[2,64,256]{2,1,0:T(8,128)S(1)} %get-tuple-element.36), channel_id=1, source_target_pairs={{0,128},{1,129},{2,130},{3,131},{4,132},{5,133},{6,134},{7,135},{8... | collective-permute-start | bytes 393224 | tf_op jit(solution)/shard_map/ppermute | solution.py:46
  93.5 10.7 %collective-permute-start.36 = (f32[2,64,256]{2,1,0:T(8,128)S(1)}, f32[2,64,256]{2,1,0:T(8,128)S(1)}, u32[]{:S(2)}, u32[]{:S(2)}) collective-permute-start(f32[2,64,256]{2,1,0:T(8,128)S(1)} %get-tuple-element.35), channel_id=1, source_target_pairs={{0,192},{1,193},{2,194},{3,195},{4,196},{5,197},{6,198},{7,199},{8... | collective-permute-start | bytes 393224 | tf_op jit(solution)/shard_map/ppermute | solution.py:46
  96.0 6.8 %collective-permute-start.38 = (f32[128,128]{1,0:T(8,128)S(1)}, f32[128,128]{1,0:T(8,128)S(1)}, u32[]{:S(2)}, u32[]{:S(2)}) collective-permute-start(f32[128,128]{1,0:T(8,128)S(1)} %get-tuple-element.38), channel_id=1, source_target_pairs={{0,32},{1,33},{2,34},{3,35},{4,36},{5,37},{6,38},{7,39},{8,40},{9,... | collective-permute-start | bytes 196616 | tf_op jit(solution)/shard_map/ppermute | solution.py:46
  96.0 6.7 %collective-permute-start.39 = (f32[128,128]{1,0:T(8,128)S(1)}, f32[128,128]{1,0:T(8,128)S(1)}, u32[]{:S(2)}, u32[]{:S(2)}) collective-permute-start(f32[128,128]{1,0:T(8,128)S(1)} %get-tuple-element.37), channel_id=1, source_target_pairs={{0,48},{1,49},{2,50},{3,51},{4,52},{5,53},{6,54},{7,55},{8,56},{9,... | collective-permute-start | bytes 196616 | tf_op jit(solution)/shard_map/ppermute | solution.py:46
  104.2 11.3 %copy-start.3 = (f32[2,64,256]{2,1,0:T(8,128)S(1)}, f32[2,64,256]{2,1,0:T(8,128)}, u32[]{:S(2)}) copy-start(f32[2,64,256]{2,1,0:T(8,128)} %param.7) | copy-start | bytes 393220
  104.3 11.3 %collective-permute-start.40 = (f32[2,64,256]{2,1,0:T(8,128)S(1)}, f32[2,64,256]{2,1,0:T(8,128)S(1)}, u32[]{:S(2)}, u32[]{:S(2)}) collective-permute-start(f32[2,64,256]{2,1,0:T(8,128)S(1)} %fusion.2), channel_id=1, source_target_pairs={{0,0},{1,32},{2,2},{3,34},{4,4},{5,36},{6,6},{7,38},{8,1},{9,33},{... | collective-permute-start | bytes 393224 | tf_op jit(solution)/shard_map/ppermute | solution.py:46
where the time goes:
time: 116 us
  starting transfers between devices  55 us (47%)
  waiting for transfers between devices  49.8 us (43%)
  Pallas kernels  7.94 us (7%)
  local copies, waits for them, and re-layouts  1.73 us (1%)
    ppermute x41, starting transfers between devices, send(): return lax.ppermute(value, AX, pairs)  55 us
    ppermute x41, waiting for transfers between devices, send(): return lax.ppermute(value, AX, pairs)  49.8 us
    pallas_call x4, Pallas kernels, local_call(): pl.pallas_call(kernel, out_shape=[jax.ShapeDtypeStruct(s, jnp.float32) fo...  7.94 us
  transfers between devices with their start and end apart: 41, of which 19 were waited for; matrix products, arithmetic and copies ran while one was open for 0% of the time, Pallas kernels for 4%

commit v1 on v0

--- a/solution.py
+++ b/solution.py
@@ -173,8 +173,8 @@
     )
     strips[3], root1 = lax.optimization_barrier((strips[3], root1))
     column = jnp.stack([strips[0]] + [send(strips[d], Z_MOVES[d]) for d in (1, 2, 3)])
-    own = [send(column, CROSS[t]) for t in range(4)]
-    other = [send(v, CORE) for v in own]
+    own = [send(column, CROSS[t]) for t in (3, 2, 1, 0)][::-1]
+    other = [send(v, CORE) for v in own[::-1]][::-1]
     around1 = step((factor, factor))
     root2 = step(root1)
     root3 = step(root2)
@@ -210,11 +210,11 @@
     rows = [lax.dynamic_index_in_dim(g_rows, (zl + d) & 3, 0, keepdims=False) for d in range(4)]
     rows = [rows[0]] + [send(rows[d], Z_MOVES[d]) for d in (1, 2, 3)]
     swapped = send(out_send, CORE)
-    (cross,) = local_call(output_kernel, [at, pattern], rows, [(2, BLK, cols)], [pltpu.VMEM((4,) + piece, jnp.float32)], 2**16, 2**20)
     part = out_keep + swapped
     last = part[0] + send(part[1], X_MOVES[1]) + send(part[2], X_MOVES[2]) + send(part[3], X_MOVES[3])
-    last, cross = lax.optimization_barrier((last, cross))
+    last, rows[1], rows[2] = lax.optimization_barrier((last, rows[1], rows[2]))
     diag = diag_inverse + send(last, HOME)
+    (cross,) = local_call(output_kernel, [at, pattern], rows, [(2, BLK, cols)], [pltpu.VMEM((4,) + piece, jnp.float32)], 2**16, 2**20)
     return cross, diag
 
 

time: 116 us -> 116 us (level)
  the two profiles are of different devices: /device:TPU:98 before, /device:TPU:72 now
where the time goes in v1:
time: 116 us
  starting transfers between devices  65 us (56%)
  waiting for transfers between devices  39.8 us (34%)
  Pallas kernels  7.94 us (7%)
  local copies, waits for them, and re-layouts  1.72 us (1%)
    ppermute x41, starting transfers between devices, send(): return lax.ppermute(value, AX, pairs)  65 us
    ppermute x41, waiting for transfers between devices, send(): return lax.ppermute(value, AX, pairs)  39.8 us
    pallas_call x4, Pallas kernels, local_call(): pl.pallas_call(kernel, out_shape=[jax.ShapeDtypeStruct(s, jnp.float32) fo...  7.94 us
  transfers between devices with their start and end apart: 41, of which 18 were waited for; matrix products, arithmetic and copies ran while one was open for 0% of the time, Pallas kernels for 4%

profile of v1, /device:TPU:72, one launch (start us, length us, event | category | flops | bytes accessed | tf_op | source)
XLA Modules:
  0.0 116.1 jit_solution(16639371872365048222)
XLA Ops:
  0.6 2.0 %collective-permute-start = (f32[128,512]{1,0:T(8,128)}, f32[128,512]{1,0:T(8,128)S(1)}, u32[]{:S(2)}, u32[]{:S(2)}) collective-permute-start(f32[128,512]{1,0:T(8,128)} %r0.1), channel_id=1, source_target_pairs={{0,16},{1,17},{2,18},{3,19},{4,20},{5,21},{6,22},{7,23},{8,24},{9,... | collective-permute-start | bytes 786440 | tf_op jit(solution)/shard_map/ppermute | solution.py:46
  2.6 0.1 collective-permute-start.1
  2.7 0.1 stack.42.at
  2.8 0.6 copy-done.1
  3.4 0.9 copy-done
  4.4 0.7 shard_map.59
  5.1 3.1 %collective-permute-start.8 = (f32[128,128]{1,0:T(8,128)S(1)}, f32[128,128]{1,0:T(8,128)S(1)}, u32[]{:S(2)}, u32[]{:S(2)}) collective-permute-start(f32[128,128]{1,0:T(8,128)S(1)} %get-tuple-element.23), channel_id=1, source_target_pairs={{0,16},{1,17},{2,18},{3,19},{4,20},{5,21},{6,22},{7,23},{8,24},{9,... | collective-permute-start | bytes 196616 | tf_op jit(solution)/shard_map/ppermute | solution.py:46
  8.2 0.7 collective-permute-start.9
  8.8 0.8 collective-permute-done.r7
  9.7 3.5 %collective-permute-done.1.r1 = f32[128,512]{1,0:T(8,128)S(1)} collective-permute-done((f32[128,512]{1,0:T(8,128)}, f32[128,512]{1,0:T(8,128)S(1)}, u32[]{:S(2)}, u32[]{:S(2)}) %collective-permute-start.1) | collective-permute-done | bytes 262176 | tf_op jit(solution)/shard_map/ppermute | solution.py:46
  13.2 2.0 %collective-permute-start.25 = (f32[128,512]{1,0:T(8,128)S(1)}, f32[128,512]{1,0:T(8,128)S(1)}, u32[]{:S(2)}, u32[]{:S(2)}) collective-permute-start(f32[128,512]{1,0:T(8,128)S(1)} %get-tuple-element.30.e0), channel_id=1, source_target_pairs={{0,16},{1,17},{2,18},{3,19},{4,20},{5,21},{6,22},{7,23},{8,24},{9,... | collective-permute-start | bytes 786440 | tf_op jit(solution)/shard_map/ppermute | solution.py:46
  15.2 2.0 %collective-permute-start.4 = (f32[128,512]{1,0:T(8,128)S(1)}, f32[128,512]{1,0:T(8,128)S(1)}, u32[]{:S(2)}, u32[]{:S(2)}) collective-permute-start(f32[128,512]{1,0:T(8,128)S(1)} %collective-permute-done.r7), channel_id=1, source_target_pairs={{0,16},{1,17},{2,18},{3,19},{4,20},{5,21},{6,22},{7,23},{8,24},{9,... | collective-permute-start | bytes 786440 | tf_op jit(solution)/shard_map/ppermute | solution.py:46
  17.2 0.0 collective-permute-done.8
  17.3 0.2 collective-permute-done.10
  17.5 0.0 copy-start.2
  17.5 3.4 %collective-permute-start.11 = (f32[4,128,128]{2,1,0:T(8,128)S(1)}, f32[4,128,128]{2,1,0:T(8,128)S(1)}, u32[]{:S(2)}, u32[]{:S(2)}) collective-permute-start(f32[4,128,128]{2,1,0:T(8,128)S(1)} %pad_maximum_fusion), channel_id=1, source_target_pairs={{0,0},{1,1},{2,64},{3,65},{4,128},{5,129},{6,192},{7,193},{8,8},{9... | collective-permute-start | bytes 786440 | tf_op jit(solution)/shard_map/ppermute | solution.py:46
  20.9 4.7 %collective-permute-start.12 = (f32[4,128,128]{2,1,0:T(8,128)S(1)}, f32[4,128,128]{2,1,0:T(8,128)S(1)}, u32[]{:S(2)}, u32[]{:S(2)}) collective-permute-start(f32[4,128,128]{2,1,0:T(8,128)S(1)} %pad_maximum_fusion), channel_id=1, source_target_pairs={{0,64},{1,65},{2,128},{3,129},{4,192},{5,193},{6,0},{7,1},{8,72},{... | collective-permute-start | bytes 786440 | tf_op jit(solution)/shard_map/ppermute | solution.py:46
  25.6 0.0 collective-permute-done.25.e7
  25.6 3.2 %collective-permute-start.13 = (f32[4,128,128]{2,1,0:T(8,128)S(1)}, f32[4,128,128]{2,1,0:T(8,128)S(1)}, u32[]{:S(2)}, u32[]{:S(2)}) collective-permute-start(f32[4,128,128]{2,1,0:T(8,128)S(1)} %pad_maximum_fusion), channel_id=1, source_target_pairs={{0,128},{1,129},{2,192},{3,193},{4,0},{5,1},{6,64},{7,65},{8,136},... | collective-permute-start | bytes 786440 | tf_op jit(solution)/shard_map/ppermute | solution.py:46
  28.9 0.0 collective-permute-done.4.r6
  28.9 4.4 %collective-permute-start.5 = (f32[128,512]{1,0:T(8,128)S(1)}, f32[128,512]{1,0:T(8,128)S(1)}, u32[]{:S(2)}, u32[]{:S(2)}) collective-permute-start(f32[128,512]{1,0:T(8,128)S(1)} %collective-permute-done.4.r6), channel_id=1, source_target_pairs={{0,16},{1,17},{2,18},{3,19},{4,20},{5,21},{6,22},{7,23},{8,24},{9,... | collective-permute-start | bytes 786440 | tf_op jit(solution)/shard_map/ppermute | solution.py:46
  33.3 5.0 %collective-permute-done.12.o1 = f32[4,128,128]{2,1,0:T(8,128)S(1)} collective-permute-done((f32[4,128,128]{2,1,0:T(8,128)S(1)}, f32[4,128,128]{2,1,0:T(8,128)S(1)}, u32[]{:S(2)}, u32[]{:S(2)}) %collective-permute-start.12) | collective-permute-done | bytes 262176 | tf_op jit(solution)/shard_map/ppermute | solution.py:46
  38.3 2.1 %collective-permute-start.22 = (f32[128,512]{1,0:T(8,128)S(1)}, f32[128,512]{1,0:T(8,128)S(1)}, u32[]{:S(2)}, u32[]{:S(2)}) collective-permute-start(f32[128,512]{1,0:T(8,128)S(1)} %get-tuple-element.30.e0), channel_id=1, source_target_pairs={{0,49},{1,48},{2,51},{3,50},{4,53},{5,52},{6,55},{7,54},{8,57},{9,... | collective-permute-start | bytes 786440 | tf_op jit(solution)/shard_map/ppermute | solution.py:46
  40.5 0.5 collective-permute-start.16
  41.0 0.3 collective-permute-start.17
  41.2 1.0 collective-permute-done.3.r3
  42.3 4.0 %collective-permute-done.22.e1 = f32[128,512]{1,0:T(8,128)S(1)} collective-permute-done((f32[128,512]{1,0:T(8,128)S(1)}, f32[128,512]{1,0:T(8,128)S(1)}, u32[]{:S(2)}, u32[]{:S(2)}) %collective-permute-start.22) | collective-permute-done | bytes 262176 | tf_op jit(solution)/shard_map/ppermute | solution.py:46
  46.3 3.2 %collective-permute-start.6 = (f32[64,512]{1,0:T(8,128)S(1)}, f32[64,512]{1,0:T(8,128)S(1)}, u32[]{:S(2)}, u32[]{:S(2)}) collective-permute-start(f32[64,512]{1,0:T(8,128)S(1)} %slice.32), channel_id=1, source_target_pairs={{0,16},{1,17},{2,18},{3,19},{4,20},{5,21},{6,22},{7,23},{8,24},{9,... | collective-permute-start | bytes 393224 | tf_op jit(solution)/shard_map/ppermute | solution.py:46
  49.5 2.0 %collective-permute-start.26 = (f32[128,512]{1,0:T(8,128)S(1)}, f32[128,512]{1,0:T(8,128)S(1)}, u32[]{:S(2)}, u32[]{:S(2)}) collective-permute-start(f32[128,512]{1,0:T(8,128)S(1)} %collective-permute-done.25.e7), channel_id=1, source_target_pairs={{0,16},{1,17},{2,18},{3,19},{4,20},{5,21},{6,22},{7,23},{8,24},{9,... | collective-permute-start | bytes 786440 | tf_op jit(solution)/shard_map/ppermute | solution.py:46
  51.6 0.1 collective-permute-start.23
  51.6 0.8 collective-permute-done.6.r4t
  52.5 2.0 %collective-permute-done.7.r4b = f32[64,512]{1,0:T(8,128)S(1)} collective-permute-done((f32[64,512]{1,0:T(8,128)S(1)}, f32[64,512]{1,0:T(8,128)S(1)}, u32[]{:S(2)}, u32[]{:S(2)}) %collective-permute-start.7) | collective-permute-done | bytes 131104 | tf_op jit(solution)/shard_map/ppermute | solution.py:46
  54.5 2.9 %shard_map.60 = (f32[512,128]{1,0:T(8,128)S(1)}, f32[512,128]{1,0:T(8,128)S(1)}, f32[512,128]{1,0:T(8,128)S(1)}, f32[512,128]{1,0:T(8,128)S(1)}) custom-call(s32[6]{0:T(128)S(1)} %stack.42.at, f32[128,512]{1,0:T(8,128)S(1)} %copy-done.2, f32[128,512]{1,0:T(8,128)S(1)} %collective-permute-done.1.r1, f32[128,512]{1,0:T(8,128)S(1)} %collective-permute-done.2.r2, ...), custom_call_target="tpu_custom_call" | custom-call | flops 1610612736 | bytes 6291456 | tf_op jit(solution)/shard_map/pallas_call | solution.py:152
  57.5 0.1 collective-permute-start.19
  57.5 5.9 %collective-permute-start.20 = (f32[512,128]{1,0:T(8,128)S(1)}, f32[512,128]{1,0:T(8,128)S(1)}, u32[]{:S(2)}, u32[]{:S(2)}) collective-permute-start(f32[512,128]{1,0:T(8,128)S(1)} %get-tuple-element.28), channel_id=1, source_target_pairs={{0,4},{1,5},{2,6},{3,7},{4,0},{5,1},{6,2},{7,3},{8,12},{9,13},{10,... | collective-permute-start | bytes 786440 | tf_op jit(solution)/shard_map/ppermute | solution.py:46
  63.5 2.5 %collective-permute-start.21 = (f32[512,128]{1,0:T(8,128)S(1)}, f32[512,128]{1,0:T(8,128)S(1)}, u32[]{:S(2)}, u32[]{:S(2)}) collective-permute-start(f32[512,128]{1,0:T(8,128)S(1)} %get-tuple-element.29), channel_id=1, source_target_pairs={{0,6},{1,7},{2,0},{3,1},{4,2},{5,3},{6,4},{7,5},{8,14},{9,15},{10,... | collective-permute-start | bytes 786440 | tf_op jit(solution)/shard_map/ppermute | solution.py:46
  66.0 1.7 %collective-permute-start.27 = (f32[128,512]{1,0:T(8,128)S(1)}, f32[128,512]{1,0:T(8,128)S(1)}, u32[]{:S(2)}, u32[]{:S(2)}) collective-permute-start(f32[128,512]{1,0:T(8,128)S(1)} %collective-permute-done.26.e6), channel_id=1, source_target_pairs={{0,16},{1,17},{2,18},{3,19},{4,20},{5,21},{6,22},{7,23},{8,24},{9,... | collective-permute-start | bytes 786440 | tf_op jit(solution)/shard_map/ppermute | solution.py:46
  67.7 0.3 collective-permute-start.24
  68.0 0.7 collective-permute-done.20
  68.7 2.7 %collective-permute-done.21 = f32[512,128]{1,0:T(8,128)S(1)} collective-permute-done((f32[512,128]{1,0:T(8,128)S(1)}, f32[512,128]{1,0:T(8,128)S(1)}, u32[]{:S(2)}, u32[]{:S(2)}) %collective-permute-start.21) | collective-permute-done | bytes 262176 | tf_op jit(solution)/shard_map/ppermute | solution.py:46
  71.4 1.5 %collective-permute-start.30 = (f32[512,128]{1,0:T(8,128)S(1)}, f32[512,128]{1,0:T(8,128)S(1)}, u32[]{:S(2)}, u32[]{:S(2)}) collective-permute-start(f32[512,128]{1,0:T(8,128)S(1)} %add_add_fusion.g0), channel_id=1, source_target_pairs={{0,2},{1,3},{2,4},{3,5},{4,6},{5,7},{6,0},{7,1},{8,10},{9,11},{10,... | collective-permute-start | bytes 786440 | tf_op jit(solution)/shard_map/ppermute | solution.py:46
  72.9 3.6 %collective-permute-start.31 = (f32[512,128]{1,0:T(8,128)S(1)}, f32[512,128]{1,0:T(8,128)S(1)}, u32[]{:S(2)}, u32[]{:S(2)}) collective-permute-start(f32[512,128]{1,0:T(8,128)S(1)} %add_add_fusion.g0), channel_id=1, source_target_pairs={{0,4},{1,5},{2,6},{3,7},{4,0},{5,1},{6,2},{7,3},{8,12},{9,13},{10,... | collective-permute-start | bytes 786440 | tf_op jit(solution)/shard_map/ppermute | solution.py:46
  76.5 1.2 %collective-permute-start.32 = (f32[512,128]{1,0:T(8,128)S(1)}, f32[512,128]{1,0:T(8,128)S(1)}, u32[]{:S(2)}, u32[]{:S(2)}) collective-permute-start(f32[512,128]{1,0:T(8,128)S(1)} %add_add_fusion.g0), channel_id=1, source_target_pairs={{0,6},{1,7},{2,0},{3,1},{4,2},{5,3},{6,4},{7,5},{8,14},{9,15},{10,... | collective-permute-start | bytes 786440 | tf_op jit(solution)/shard_map/ppermute | solution.py:46
  77.8 1.9 %collective-permute-start.28 = (f32[64,512]{1,0:T(8,128)S(1)}, f32[64,512]{1,0:T(8,128)S(1)}, u32[]{:S(2)}, u32[]{:S(2)}) collective-permute-start(f32[64,512]{1,0:T(8,128)S(1)} %slice.34), channel_id=1, source_target_pairs={{0,16},{1,17},{2,18},{3,19},{4,20},{5,21},{6,22},{7,23},{8,24},{9,... | collective-permute-start | bytes 393224 | tf_op jit(solution)/shard_map/ppermute | solution.py:46
  79.7 1.4 %collective-permute-start.29 = (f32[64,512]{1,0:T(8,128)S(1)}, f32[64,512]{1,0:T(8,128)S(1)}, u32[]{:S(2)}, u32[]{:S(2)}) collective-permute-start(f32[64,512]{1,0:T(8,128)S(1)} %slice.35), channel_id=1, source_target_pairs={{0,49},{1,48},{2,51},{3,50},{4,53},{5,52},{6,55},{7,54},{8,57},{9,... | collective-permute-start | bytes 393224 | tf_op jit(solution)/shard_map/ppermute | solution.py:46
  81.1 2.8 %collective-permute-done.28.e4t = f32[64,512]{1,0:T(8,128)S(1)} collective-permute-done((f32[64,512]{1,0:T(8,128)S(1)}, f32[64,512]{1,0:T(8,128)S(1)}, u32[]{:S(2)}, u32[]{:S(2)}) %collective-permute-start.28) | collective-permute-done | bytes 131104 | tf_op jit(solution)/shard_map/ppermute | solution.py:46
  84.0 0.8 collective-permute-done.29.e4b
  84.8 2.8 %shard_map.61 = (f32[4,2,64,256]{3,2,1,0:T(8,128)S(1)}, f32[4,2,64,256]{3,2,1,0:T(8,128)S(1)}) custom-call(s32[6]{0:T(128)S(1)} %stack.42.at, f32[128,512]{1,0:T(8,128)S(1)} %get-tuple-element.30.e0, f32[128,512]{1,0:T(8,128)S(1)} %collective-permute-done.22.e1, f32[128,512]{1,0:T(8,128)S(1)} %collective-permute-done.23.e2, ...), custom_call_target="tpu_custom_call" | custom-call | flops 805306368 | bytes 6291456 | tf_op jit(solution)/shard_map/pallas_call | solution.py:152
  87.6 0.1 collective-permute-start.33
  87.7 1.9 %collective-permute-done.33 = f32[4,2,64,256]{3,2,1,0:T(8,128)S(1)} collective-permute-done((f32[4,2,64,256]{3,2,1,0:T(8,128)S(1)}, f32[4,2,64,256]{3,2,1,0:T(8,128)S(1)}, u32[]{:S(2)}, u32[]{:S(2)}) %collective-permute-start.33) | collective-permute-done | bytes 524320 | tf_op jit(solution)/shard_map/ppermute | solution.py:46
  89.6 0.1 add.54
  89.7 0.1 collective-permute-start.34
  89.8 6.2 %collective-permute-start.35 = (f32[2,64,256]{2,1,0:T(8,128)S(1)}, f32[2,64,256]{2,1,0:T(8,128)S(1)}, u32[]{:S(2)}, u32[]{:S(2)}) collective-permute-start(f32[2,64,256]{2,1,0:T(8,128)S(1)} %get-tuple-element.38), channel_id=1, source_target_pairs={{0,128},{1,129},{2,130},{3,131},{4,132},{5,133},{6,134},{7,135},{8... | collective-permute-start | bytes 393224 | tf_op jit(solution)/shard_map/ppermute | solution.py:46
  96.1 1.3 %collective-permute-start.37 = (f32[128,128]{1,0:T(8,128)S(1)}, f32[128,128]{1,0:T(8,128)S(1)}, u32[]{:S(2)}, u32[]{:S(2)}) collective-permute-start(f32[128,128]{1,0:T(8,128)S(1)} %get-tuple-element.41), channel_id=1, source_target_pairs={{0,16},{1,17},{2,18},{3,19},{4,20},{5,21},{6,22},{7,23},{8,24},{9,... | collective-permute-start | bytes 196616 | tf_op jit(solution)/shard_map/ppermute | solution.py:46
  97.4 0.2 collective-permute-start.38
  97.7 0.7 collective-permute-done.34
  98.4 4.0 %collective-permute-done.35 = f32[2,64,256]{2,1,0:T(8,128)S(1)} collective-permute-done((f32[2,64,256]{2,1,0:T(8,128)S(1)}, f32[2,64,256]{2,1,0:T(8,128)S(1)}, u32[]{:S(2)}, u32[]{:S(2)}) %collective-permute-start.35) | collective-permute-done | bytes 131104 | tf_op jit(solution)/shard_map/ppermute | solution.py:46
  102.4 0.2 collective-permute-done.38.a2
  102.6 2.7 %collective-permute-start.40 = (f32[2,64,256]{2,1,0:T(8,128)S(1)}, f32[2,64,256]{2,1,0:T(8,128)S(1)}, u32[]{:S(2)}, u32[]{:S(2)}) collective-permute-start(f32[2,64,256]{2,1,0:T(8,128)S(1)} %fusion.2), channel_id=1, source_target_pairs={{0,0},{1,32},{2,2},{3,34},{4,4},{5,36},{6,6},{7,38},{8,1},{9,33},{... | collective-permute-start | bytes 393224 | tf_op jit(solution)/shard_map/ppermute | solution.py:46
  105.4 0.1 collective-permute-start.39
  105.5 6.6 %collective-permute-done.39.a3 = f32[128,128]{1,0:T(8,128)S(1)} collective-permute-done((f32[128,128]{1,0:T(8,128)S(1)}, f32[128,128]{1,0:T(8,128)S(1)}, u32[]{:S(2)}, u32[]{:S(2)}) %collective-permute-start.39) | collective-permute-done | bytes 65568 | tf_op jit(solution)/shard_map/ppermute | solution.py:46
  112.1 1.4 %shard_map.62 = f32[2,128,256]{2,1,0:T(8,128)} custom-call(s32[6]{0:T(128)S(1)} %stack.42.at, s32[2,32]{1,0:T(2,128)S(1)} %copy-done.1, f32[128,128]{1,0:T(8,128)S(1)} %get-tuple-element.42.a0, f32[128,128]{1,0:T(8,128)S(1)} %collective-permute-done.37.a1, f32[128,128]{1,0:T(8,128)S(1)} %collective-permute-done.38.a2, f32[128,128]{1,0:T(8,128)S(1)} %collective-permute-done.39.a3), custom_call_target="tpu_custom_call" | custom-call | flops 65536 | bytes 1048576 | tf_op jit(solution)/shard_map/pallas_call | solution.py:152
  113.5 1.9 %collective-permute-done.40 = f32[2,64,256]{2,1,0:T(8,128)S(1)} collective-permute-done((f32[2,64,256]{2,1,0:T(8,128)S(1)}, f32[2,64,256]{2,1,0:T(8,128)S(1)}, u32[]{:S(2)}, u32[]{:S(2)}) %collective-permute-start.40) | collective-permute-done | bytes 131104 | tf_op jit(solution)/shard_map/ppermute | solution.py:46
  115.5 0.7 add.64
  (42 shorter events, 0.3 us)
Async XLA Ops:
  0.6 9.0 %collective-permute-start = (f32[128,512]{1,0:T(8,128)}, f32[128,512]{1,0:T(8,128)S(1)}, u32[]{:S(2)}, u32[]{:S(2)}) collective-permute-start(f32[128,512]{1,0:T(8,128)} %r0.1), channel_id=1, source_target_pairs={{0,16},{1,17},{2,18},{3,19},{4,20},{5,21},{6,22},{7,23},{8,24},{9,... | collective-permute-start | bytes 786440 | tf_op jit(solution)/shard_map/ppermute | solution.py:46
  2.6 10.5 %collective-permute-start.1 = (f32[128,512]{1,0:T(8,128)}, f32[128,512]{1,0:T(8,128)S(1)}, u32[]{:S(2)}, u32[]{:S(2)}) collective-permute-start(f32[128,512]{1,0:T(8,128)} %r0.1), channel_id=1, source_target_pairs={{0,49},{1,48},{2,51},{3,50},{4,53},{5,52},{6,55},{7,54},{8,57},{9,... | collective-permute-start | bytes 786440 | tf_op jit(solution)/shard_map/ppermute | solution.py:46
  2.7 0.7 copy-start.1
  3.4 0.9 copy-start
  5.1 12.2 %collective-permute-start.8 = (f32[128,128]{1,0:T(8,128)S(1)}, f32[128,128]{1,0:T(8,128)S(1)}, u32[]{:S(2)}, u32[]{:S(2)}) collective-permute-start(f32[128,128]{1,0:T(8,128)S(1)} %get-tuple-element.23), channel_id=1, source_target_pairs={{0,16},{1,17},{2,18},{3,19},{4,20},{5,21},{6,22},{7,23},{8,24},{9,... | collective-permute-start | bytes 196616 | tf_op jit(solution)/shard_map/ppermute | solution.py:46
  8.2 9.1 %collective-permute-start.9 = (f32[128,128]{1,0:T(8,128)S(1)}, f32[128,128]{1,0:T(8,128)S(1)}, u32[]{:S(2)}, u32[]{:S(2)}) collective-permute-start(f32[128,128]{1,0:T(8,128)S(1)} %get-tuple-element.24), channel_id=1, source_target_pairs={{0,32},{1,33},{2,34},{3,35},{4,36},{5,37},{6,38},{7,39},{8,40},{9,... | collective-permute-start | bytes 196616 | tf_op jit(solution)/shard_map/ppermute | solution.py:46
  13.2 4.3 %collective-permute-start.10 = (f32[128,128]{1,0:T(8,128)S(1)}, f32[128,128]{1,0:T(8,128)S(1)}, u32[]{:S(2)}, u32[]{:S(2)}) collective-permute-start(f32[128,128]{1,0:T(8,128)S(1)} %get-tuple-element.25), channel_id=1, source_target_pairs={{0,48},{1,49},{2,50},{3,51},{4,52},{5,53},{6,54},{7,55},{8,56},{9,... | collective-permute-start | bytes 196616 | tf_op jit(solution)/shard_map/ppermute | solution.py:46
  13.2 12.5 %collective-permute-start.25 = (f32[128,512]{1,0:T(8,128)S(1)}, f32[128,512]{1,0:T(8,128)S(1)}, u32[]{:S(2)}, u32[]{:S(2)}) collective-permute-start(f32[128,512]{1,0:T(8,128)S(1)} %get-tuple-element.30.e0), channel_id=1, source_target_pairs={{0,16},{1,17},{2,18},{3,19},{4,20},{5,21},{6,22},{7,23},{8,24},{9,... | collective-permute-start | bytes 786440 | tf_op jit(solution)/shard_map/ppermute | solution.py:46
  15.2 13.7 %collective-permute-start.4 = (f32[128,512]{1,0:T(8,128)S(1)}, f32[128,512]{1,0:T(8,128)S(1)}, u32[]{:S(2)}, u32[]{:S(2)}) collective-permute-start(f32[128,512]{1,0:T(8,128)S(1)} %collective-permute-done.r7), channel_id=1, source_target_pairs={{0,16},{1,17},{2,18},{3,19},{4,20},{5,21},{6,22},{7,23},{8,24},{9,... | collective-permute-start | bytes 786440 | tf_op jit(solution)/shard_map/ppermute | solution.py:46
  17.2 11.7 %collective-permute-start.2 = (f32[128,512]{1,0:T(8,128)S(1)}, f32[128,512]{1,0:T(8,128)S(1)}, u32[]{:S(2)}, u32[]{:S(2)}) collective-permute-start(f32[128,512]{1,0:T(8,128)S(1)} %collective-permute-done.1.r1), channel_id=1, source_target_pairs={{0,49},{1,48},{2,51},{3,50},{4,53},{5,52},{6,55},{7,54},{8,57},{9,... | collective-permute-start | bytes 786440 | tf_op jit(solution)/shard_map/ppermute | solution.py:46
  17.5 37.0 %copy-start.2 = (f32[128,512]{1,0:T(8,128)S(1)}, f32[128,512]{1,0:T(8,128)}, u32[]{:S(2)}) copy-start(f32[128,512]{1,0:T(8,128)} %r0.1) | copy-start | bytes 786436
  17.5 15.9 %collective-permute-start.11 = (f32[4,128,128]{2,1,0:T(8,128)S(1)}, f32[4,128,128]{2,1,0:T(8,128)S(1)}, u32[]{:S(2)}, u32[]{:S(2)}) collective-permute-start(f32[4,128,128]{2,1,0:T(8,128)S(1)} %pad_maximum_fusion), channel_id=1, source_target_pairs={{0,0},{1,1},{2,64},{3,65},{4,128},{5,129},{6,192},{7,193},{8,8},{9... | collective-permute-start | bytes 786440 | tf_op jit(solution)/shard_map/ppermute | solution.py:46
  20.9 17.5 %collective-permute-start.12 = (f32[4,128,128]{2,1,0:T(8,128)S(1)}, f32[4,128,128]{2,1,0:T(8,128)S(1)}, u32[]{:S(2)}, u32[]{:S(2)}) collective-permute-start(f32[4,128,128]{2,1,0:T(8,128)S(1)} %pad_maximum_fusion), channel_id=1, source_target_pairs={{0,64},{1,65},{2,128},{3,129},{4,192},{5,193},{6,0},{7,1},{8,72},{... | collective-permute-start | bytes 786440 | tf_op jit(solution)/shard_map/ppermute | solution.py:46
  25.6 14.8 %collective-permute-start.13 = (f32[4,128,128]{2,1,0:T(8,128)S(1)}, f32[4,128,128]{2,1,0:T(8,128)S(1)}, u32[]{:S(2)}, u32[]{:S(2)}) collective-permute-start(f32[4,128,128]{2,1,0:T(8,128)S(1)} %pad_maximum_fusion), channel_id=1, source_target_pairs={{0,128},{1,129},{2,192},{3,193},{4,0},{5,1},{6,64},{7,65},{8,136},... | collective-permute-start | bytes 786440 | tf_op jit(solution)/shard_map/ppermute | solution.py:46
  28.9 11.6 %collective-permute-start.14 = (f32[4,128,128]{2,1,0:T(8,128)S(1)}, f32[4,128,128]{2,1,0:T(8,128)S(1)}, u32[]{:S(2)}, u32[]{:S(2)}) collective-permute-start(f32[4,128,128]{2,1,0:T(8,128)S(1)} %pad_maximum_fusion), channel_id=1, source_target_pairs={{0,192},{1,193},{2,0},{3,1},{4,64},{5,65},{6,128},{7,129},{8,200},... | collective-permute-start | bytes 786440 | tf_op jit(solution)/shard_map/ppermute | solution.py:46
  28.9 12.1 %collective-permute-start.5 = (f32[128,512]{1,0:T(8,128)S(1)}, f32[128,512]{1,0:T(8,128)S(1)}, u32[]{:S(2)}, u32[]{:S(2)}) collective-permute-start(f32[128,512]{1,0:T(8,128)S(1)} %collective-permute-done.4.r6), channel_id=1, source_target_pairs={{0,16},{1,17},{2,18},{3,19},{4,20},{5,21},{6,22},{7,23},{8,24},{9,... | collective-permute-start | bytes 786440 | tf_op jit(solution)/shard_map/ppermute | solution.py:46
  33.3 8.9 %collective-permute-start.3 = (f32[128,512]{1,0:T(8,128)S(1)}, f32[128,512]{1,0:T(8,128)S(1)}, u32[]{:S(2)}, u32[]{:S(2)}) collective-permute-start(f32[128,512]{1,0:T(8,128)S(1)} %collective-permute-done.2.r2), channel_id=1, source_target_pairs={{0,49},{1,48},{2,51},{3,50},{4,53},{5,52},{6,55},{7,54},{8,57},{9,... | collective-permute-start | bytes 786440 | tf_op jit(solution)/shard_map/ppermute | solution.py:46
  38.3 7.9 %collective-permute-start.22 = (f32[128,512]{1,0:T(8,128)S(1)}, f32[128,512]{1,0:T(8,128)S(1)}, u32[]{:S(2)}, u32[]{:S(2)}) collective-permute-start(f32[128,512]{1,0:T(8,128)S(1)} %get-tuple-element.30.e0), channel_id=1, source_target_pairs={{0,49},{1,48},{2,51},{3,50},{4,53},{5,52},{6,55},{7,54},{8,57},{9,... | collective-permute-start | bytes 786440 | tf_op jit(solution)/shard_map/ppermute | solution.py:46
  40.4 9.1 %collective-permute-start.15 = (f32[4,128,128]{2,1,0:T(8,128)S(1)}, f32[4,128,128]{2,1,0:T(8,128)S(1)}, u32[]{:S(2)}, u32[]{:S(2)}) collective-permute-start(f32[4,128,128]{2,1,0:T(8,128)S(1)} %collective-permute-done.11.o0), channel_id=1, source_target_pairs={{0,8},{1,9},{2,10},{3,11},{4,12},{5,13},{6,14},{7,15},{8,0},{9,1},... | collective-permute-start | bytes 786440 | tf_op jit(solution)/shard_map/ppermute | solution.py:46
  40.5 9.1 %collective-permute-start.16 = (f32[4,128,128]{2,1,0:T(8,128)S(1)}, f32[4,128,128]{2,1,0:T(8,128)S(1)}, u32[]{:S(2)}, u32[]{:S(2)}) collective-permute-start(f32[4,128,128]{2,1,0:T(8,128)S(1)} %collective-permute-done.12.o1), channel_id=1, source_target_pairs={{0,8},{1,9},{2,10},{3,11},{4,12},{5,13},{6,14},{7,15},{8,0},{9,1},... | collective-permute-start | bytes 786440 | tf_op jit(solution)/shard_map/ppermute | solution.py:46
  41.0 10.6 %collective-permute-start.17 = (f32[4,128,128]{2,1,0:T(8,128)S(1)}, f32[4,128,128]{2,1,0:T(8,128)S(1)}, u32[]{:S(2)}, u32[]{:S(2)}) collective-permute-start(f32[4,128,128]{2,1,0:T(8,128)S(1)} %collective-permute-done.13.o2), channel_id=1, source_target_pairs={{0,8},{1,9},{2,10},{3,11},{4,12},{5,13},{6,14},{7,15},{8,0},{9,1},... | collective-permute-start | bytes 786440 | tf_op jit(solution)/shard_map/ppermute | solution.py:46
  42.3 9.4 %collective-permute-start.18 = (f32[4,128,128]{2,1,0:T(8,128)S(1)}, f32[4,128,128]{2,1,0:T(8,128)S(1)}, u32[]{:S(2)}, u32[]{:S(2)}) collective-permute-start(f32[4,128,128]{2,1,0:T(8,128)S(1)} %collective-permute-done.14.o3), channel_id=1, source_target_pairs={{0,8},{1,9},{2,10},{3,11},{4,12},{5,13},{6,14},{7,15},{8,0},{9,1},... | collective-permute-start | bytes 786440 | tf_op jit(solution)/shard_map/ppermute | solution.py:46
  46.3 6.2 %collective-permute-start.6 = (f32[64,512]{1,0:T(8,128)S(1)}, f32[64,512]{1,0:T(8,128)S(1)}, u32[]{:S(2)}, u32[]{:S(2)}) collective-permute-start(f32[64,512]{1,0:T(8,128)S(1)} %slice.32), channel_id=1, source_target_pairs={{0,16},{1,17},{2,18},{3,19},{4,20},{5,21},{6,22},{7,23},{8,24},{9,... | collective-permute-start | bytes 393224 | tf_op jit(solution)/shard_map/ppermute | solution.py:46
  49.5 5.0 %collective-permute-start.7 = (f32[64,512]{1,0:T(8,128)S(1)}, f32[64,512]{1,0:T(8,128)S(1)}, u32[]{:S(2)}, u32[]{:S(2)}) collective-permute-start(f32[64,512]{1,0:T(8,128)S(1)} %slice.33), channel_id=1, source_target_pairs={{0,49},{1,48},{2,51},{3,50},{4,53},{5,52},{6,55},{7,54},{8,57},{9,... | collective-permute-start | bytes 393224 | tf_op jit(solution)/shard_map/ppermute | solution.py:46
  49.5 16.5 %collective-permute-start.26 = (f32[128,512]{1,0:T(8,128)S(1)}, f32[128,512]{1,0:T(8,128)S(1)}, u32[]{:S(2)}, u32[]{:S(2)}) collective-permute-start(f32[128,512]{1,0:T(8,128)S(1)} %collective-permute-done.25.e7), channel_id=1, source_target_pairs={{0,16},{1,17},{2,18},{3,19},{4,20},{5,21},{6,22},{7,23},{8,24},{9,... | collective-permute-start | bytes 786440 | tf_op jit(solution)/shard_map/ppermute | solution.py:46
  51.6 16.1 %collective-permute-start.23 = (f32[128,512]{1,0:T(8,128)S(1)}, f32[128,512]{1,0:T(8,128)S(1)}, u32[]{:S(2)}, u32[]{:S(2)}) collective-permute-start(f32[128,512]{1,0:T(8,128)S(1)} %collective-permute-done.22.e1), channel_id=1, source_target_pairs={{0,49},{1,48},{2,51},{3,50},{4,53},{5,52},{6,55},{7,54},{8,57},{9,... | collective-permute-start | bytes 786440 | tf_op jit(solution)/shard_map/ppermute | solution.py:46
  57.5 10.6 %collective-permute-start.19 = (f32[512,128]{1,0:T(8,128)S(1)}, f32[512,128]{1,0:T(8,128)S(1)}, u32[]{:S(2)}, u32[]{:S(2)}) collective-permute-start(f32[512,128]{1,0:T(8,128)S(1)} %get-tuple-element.27), channel_id=1, source_target_pairs={{0,2},{1,3},{2,4},{3,5},{4,6},{5,7},{6,0},{7,1},{8,10},{9,11},{10,... | collective-permute-start | bytes 786440 | tf_op jit(solution)/shard_map/ppermute | solution.py:46
  57.5 11.1 %collective-permute-start.20 = (f32[512,128]{1,0:T(8,128)S(1)}, f32[512,128]{1,0:T(8,128)S(1)}, u32[]{:S(2)}, u32[]{:S(2)}) collective-permute-start(f32[512,128]{1,0:T(8,128)S(1)} %get-tuple-element.28), channel_id=1, source_target_pairs={{0,4},{1,5},{2,6},{3,7},{4,0},{5,1},{6,2},{7,3},{8,12},{9,13},{10,... | collective-permute-start | bytes 786440 | tf_op jit(solution)/shard_map/ppermute | solution.py:46
  63.5 7.9 %collective-permute-start.21 = (f32[512,128]{1,0:T(8,128)S(1)}, f32[512,128]{1,0:T(8,128)S(1)}, u32[]{:S(2)}, u32[]{:S(2)}) collective-permute-start(f32[512,128]{1,0:T(8,128)S(1)} %get-tuple-element.29), channel_id=1, source_target_pairs={{0,6},{1,7},{2,0},{3,1},{4,2},{5,3},{6,4},{7,5},{8,14},{9,15},{10,... | collective-permute-start | bytes 786440 | tf_op jit(solution)/shard_map/ppermute | solution.py:46
  66.0 11.8 %collective-permute-start.27 = (f32[128,512]{1,0:T(8,128)S(1)}, f32[128,512]{1,0:T(8,128)S(1)}, u32[]{:S(2)}, u32[]{:S(2)}) collective-permute-start(f32[128,512]{1,0:T(8,128)S(1)} %collective-permute-done.26.e6), channel_id=1, source_target_pairs={{0,16},{1,17},{2,18},{3,19},{4,20},{5,21},{6,22},{7,23},{8,24},{9,... | collective-permute-start | bytes 786440 | tf_op jit(solution)/shard_map/ppermute | solution.py:46
  67.7 12.0 %collective-permute-start.24 = (f32[128,512]{1,0:T(8,128)S(1)}, f32[128,512]{1,0:T(8,128)S(1)}, u32[]{:S(2)}, u32[]{:S(2)}) collective-permute-start(f32[128,512]{1,0:T(8,128)S(1)} %collective-permute-done.23.e2), channel_id=1, source_target_pairs={{0,49},{1,48},{2,51},{3,50},{4,53},{5,52},{6,55},{7,54},{8,57},{9,... | collective-permute-start | bytes 786440 | tf_op jit(solution)/shard_map/ppermute | solution.py:46
  71.4 13.3 %collective-permute-start.30 = (f32[512,128]{1,0:T(8,128)S(1)}, f32[512,128]{1,0:T(8,128)S(1)}, u32[]{:S(2)}, u32[]{:S(2)}) collective-permute-start(f32[512,128]{1,0:T(8,128)S(1)} %add_add_fusion.g0), channel_id=1, source_target_pairs={{0,2},{1,3},{2,4},{3,5},{4,6},{5,7},{6,0},{7,1},{8,10},{9,11},{10,... | collective-permute-start | bytes 786440 | tf_op jit(solution)/shard_map/ppermute | solution.py:46
  72.9 11.9 %collective-permute-start.31 = (f32[512,128]{1,0:T(8,128)S(1)}, f32[512,128]{1,0:T(8,128)S(1)}, u32[]{:S(2)}, u32[]{:S(2)}) collective-permute-start(f32[512,128]{1,0:T(8,128)S(1)} %add_add_fusion.g0), channel_id=1, source_target_pairs={{0,4},{1,5},{2,6},{3,7},{4,0},{5,1},{6,2},{7,3},{8,12},{9,13},{10,... | collective-permute-start | bytes 786440 | tf_op jit(solution)/shard_map/ppermute | solution.py:46
  76.5 8.2 %collective-permute-start.32 = (f32[512,128]{1,0:T(8,128)S(1)}, f32[512,128]{1,0:T(8,128)S(1)}, u32[]{:S(2)}, u32[]{:S(2)}) collective-permute-start(f32[512,128]{1,0:T(8,128)S(1)} %add_add_fusion.g0), channel_id=1, source_target_pairs={{0,6},{1,7},{2,0},{3,1},{4,2},{5,3},{6,4},{7,5},{8,14},{9,15},{10,... | collective-permute-start | bytes 786440 | tf_op jit(solution)/shard_map/ppermute | solution.py:46
  77.8 6.2 %collective-permute-start.28 = (f32[64,512]{1,0:T(8,128)S(1)}, f32[64,512]{1,0:T(8,128)S(1)}, u32[]{:S(2)}, u32[]{:S(2)}) collective-permute-start(f32[64,512]{1,0:T(8,128)S(1)} %slice.34), channel_id=1, source_target_pairs={{0,16},{1,17},{2,18},{3,19},{4,20},{5,21},{6,22},{7,23},{8,24},{9,... | collective-permute-start | bytes 393224 | tf_op jit(solution)/shard_map/ppermute | solution.py:46
  79.7 5.0 %collective-permute-start.29 = (f32[64,512]{1,0:T(8,128)S(1)}, f32[64,512]{1,0:T(8,128)S(1)}, u32[]{:S(2)}, u32[]{:S(2)}) collective-permute-start(f32[64,512]{1,0:T(8,128)S(1)} %slice.35), channel_id=1, source_target_pairs={{0,49},{1,48},{2,51},{3,50},{4,53},{5,52},{6,55},{7,54},{8,57},{9,... | collective-permute-start | bytes 393224 | tf_op jit(solution)/shard_map/ppermute | solution.py:46
  87.6 2.0 %collective-permute-start.33 = (f32[4,2,64,256]{3,2,1,0:T(8,128)S(1)}, f32[4,2,64,256]{3,2,1,0:T(8,128)S(1)}, u32[]{:S(2)}, u32[]{:S(2)}) collective-permute-start(f32[4,2,64,256]{3,2,1,0:T(8,128)S(1)} %get-tuple-element.32), channel_id=1, source_target_pairs={{0,8},{1,9},{2,10},{3,11},{4,12},{5,13},{6,14},{7,15},{8,0},{9,1},... | collective-permute-start | bytes 1572872 | tf_op jit(solution)/shard_map/ppermute | solution.py:46
  89.7 8.7 %collective-permute-start.34 = (f32[2,64,256]{2,1,0:T(8,128)S(1)}, f32[2,64,256]{2,1,0:T(8,128)S(1)}, u32[]{:S(2)}, u32[]{:S(2)}) collective-permute-start(f32[2,64,256]{2,1,0:T(8,128)S(1)} %get-tuple-element.36), channel_id=1, source_target_pairs={{0,64},{1,65},{2,66},{3,67},{4,68},{5,69},{6,70},{7,71},{8,72},{9,... | collective-permute-start | bytes 393224 | tf_op jit(solution)/shard_map/ppermute | solution.py:46
  89.8 12.6 %collective-permute-start.35 = (f32[2,64,256]{2,1,0:T(8,128)S(1)}, f32[2,64,256]{2,1,0:T(8,128)S(1)}, u32[]{:S(2)}, u32[]{:S(2)}) collective-permute-start(f32[2,64,256]{2,1,0:T(8,128)S(1)} %get-tuple-element.38), channel_id=1, source_target_pairs={{0,128},{1,129},{2,130},{3,131},{4,132},{5,133},{6,134},{7,135},{8... | collective-permute-start | bytes 393224 | tf_op jit(solution)/shard_map/ppermute | solution.py:46
  96.1 6.3 %collective-permute-start.36 = (f32[2,64,256]{2,1,0:T(8,128)S(1)}, f32[2,64,256]{2,1,0:T(8,128)S(1)}, u32[]{:S(2)}, u32[]{:S(2)}) collective-permute-start(f32[2,64,256]{2,1,0:T(8,128)S(1)} %get-tuple-element.37), channel_id=1, source_target_pairs={{0,192},{1,193},{2,194},{3,195},{4,196},{5,197},{6,198},{7,199},{8... | collective-permute-start | bytes 393224 | tf_op jit(solution)/shard_map/ppermute | solution.py:46
  96.1 6.3 %collective-permute-start.37 = (f32[128,128]{1,0:T(8,128)S(1)}, f32[128,128]{1,0:T(8,128)S(1)}, u32[]{:S(2)}, u32[]{:S(2)}) collective-permute-start(f32[128,128]{1,0:T(8,128)S(1)} %get-tuple-element.41), channel_id=1, source_target_pairs={{0,16},{1,17},{2,18},{3,19},{4,20},{5,21},{6,22},{7,23},{8,24},{9,... | collective-permute-start | bytes 196616 | tf_op jit(solution)/shard_map/ppermute | solution.py:46
  97.4 5.2 %collective-permute-start.38 = (f32[128,128]{1,0:T(8,128)S(1)}, f32[128,128]{1,0:T(8,128)S(1)}, u32[]{:S(2)}, u32[]{:S(2)}) collective-permute-start(f32[128,128]{1,0:T(8,128)S(1)} %get-tuple-element.40), channel_id=1, source_target_pairs={{0,32},{1,33},{2,34},{3,35},{4,36},{5,37},{6,38},{7,39},{8,40},{9,... | collective-permute-start | bytes 196616 | tf_op jit(solution)/shard_map/ppermute | solution.py:46
  102.6 12.8 %collective-permute-start.40 = (f32[2,64,256]{2,1,0:T(8,128)S(1)}, f32[2,64,256]{2,1,0:T(8,128)S(1)}, u32[]{:S(2)}, u32[]{:S(2)}) collective-permute-start(f32[2,64,256]{2,1,0:T(8,128)S(1)} %fusion.2), channel_id=1, source_target_pairs={{0,0},{1,32},{2,2},{3,34},{4,4},{5,36},{6,6},{7,38},{8,1},{9,33},{... | collective-permute-start | bytes 393224 | tf_op jit(solution)/shard_map/ppermute | solution.py:46
  105.4 6.7 %collective-permute-start.39 = (f32[128,128]{1,0:T(8,128)S(1)}, f32[128,128]{1,0:T(8,128)S(1)}, u32[]{:S(2)}, u32[]{:S(2)}) collective-permute-start(f32[128,128]{1,0:T(8,128)S(1)} %get-tuple-element.39), channel_id=1, source_target_pairs={{0,48},{1,49},{2,50},{3,51},{4,52},{5,53},{6,54},{7,55},{8,56},{9,... | collective-permute-start | bytes 196616 | tf_op jit(solution)/shard_map/ppermute | solution.py:46
  112.1 3.4 %copy-start.3 = (f32[2,64,256]{2,1,0:T(8,128)S(1)}, f32[2,64,256]{2,1,0:T(8,128)}, u32[]{:S(2)}) copy-start(f32[2,64,256]{2,1,0:T(8,128)} %param.7) | copy-start | bytes 393220
